TPU v7x, 256 devices: a whole 4x4x8 slice. The times are simulated.
256 devices in a mesh: slab: 2 (over x_lo), sector: 64 (over x_hi, z, y), side: 2 (over core).
Axes of the slice: x: 4 (x_hi: 2, x_lo: 2; x = x_hi * 2 + x_lo), y: 4, z: 8, core: 2. Of those that a mesh axis runs over, the one named last changes fastest.
Arguments:
- traces: float32 [2, 4096, 4, 512], P('side', 'sector', None, 'slab'), may hold values from -6 to 6
- gap_gain: float32 [1024], replicated, may hold values from 0.2 to 1
- rotor_step: int32 [1], replicated, may hold values from 0 to 4095
- mixing: float32 [2, 3, 4], P('side'), may hold values from -4 to 4
- field: float32 [2, 3, 8, 4096, 512], P('side', None, None, 'sector', 'slab'), may hold values from -6 to 6
- current: float32 [2, 3, 8, 4096, 512], P('side', None, None, 'sector', 'slab'), may hold values from -6 to 6
- cond_diag: float32 [2, 3, 8, 4096, 512], P('side', None, None, 'sector', 'slab'), may hold values from 0.5 to 3
- cond_off: float32 [2, 3, 8, 4096, 512], P('side', None, None, 'sector', 'slab'), may hold values from -0.6 to 0.6
Outputs:
- new_field: float32 [2, 3, 8, 4096, 512], P('side', None, None, 'sector', 'slab')
All inputs are finite; a program needn't handle non-finite values.
Results may differ from a plain program's by a relative error of at most 0.000052.
Values sent between devices are 32-bit elements; how exact they have to be, the bound alone decides.
A program may use at most 128 MiB of HBM per device.

v0:
```python
import math

import jax
import jax.numpy as jnp
from jax import lax
from jax.sharding import PartitionSpec as P

SWEEPS = 2


HIGH = lax.Precision.HIGHEST


def partner(block, axis, bit):
    count = lax.axis_size(axis)
    route = []
    for low in range(count):
        high = low | 1 << bit
        if high != low and high < count:
            route += [(low, high), (high, low)]
    return lax.ppermute(block, axis, route)


def extended(cells, sides, width, closed):
    for axis, dim in sides:
        count = lax.axis_size(axis)
        ends = count if closed else count - 1
        head = lax.slice_in_dim(cells, 0, width, axis=dim)
        tail = lax.slice_in_dim(cells, cells.shape[dim] - width, cells.shape[dim], axis=dim)
        cells = jnp.concatenate(
            [
                lax.ppermute(tail, axis, [(i, (i + 1) % count) for i in range(ends)]),
                cells,
                lax.ppermute(head, axis, [((i + 1) % count, i) for i in range(ends)]),
            ],
            axis=dim,
        )
    return cells


def phase_angles(first, second, total):
    index = first[:, None] * second[None, :] % total
    return index.astype(jnp.float32) * (2.0 * math.pi / total)


def matmul(left, right):
    return jnp.dot(left, right, precision=HIGH, preferred_element_type=jnp.float32)


def couple(spectrum, first, gap_gain, step, sign, total):
    count = spectrum.shape[1]
    harm = first + jnp.arange(count, dtype=jnp.int32)
    angle = phase_angles(harm, jnp.reshape(step, (1,)), total)[:, 0]
    cos_r = jnp.cos(angle)[:, None, None]
    sin_r = (sign * jnp.sin(angle))[:, None, None]
    real_part, imag_part = (spectrum[0], spectrum[1])
    sent = jnp.stack([real_part * cos_r - imag_part * sin_r, imag_part * cos_r + real_part * sin_r])
    other = partner(sent, "side", 0)
    gain = lax.dynamic_slice_in_dim(gap_gain, first, count, 0)
    return spectrum + gain[None, :, None, None] * other


def inverse_terms(points, harm, total):
    angle = phase_angles(points, harm, total)
    weight = jnp.where(harm == 0, 1.0, 2.0).astype(jnp.float32) / total
    return (jnp.cos(angle) * weight[None, :], -jnp.sin(angle) * weight[None, :])


def shards(traces, gap_gain, rotor_step, mixing, field, current, cond_diag, cond_off):
    sectors = lax.axis_size("sector")
    sector_id = lax.axis_index("sector")
    side_id = lax.axis_index("side")
    local = traces[0]
    phd, comp, axd = local.shape
    nphi = phd * sectors
    nharm = gap_gain.shape[0]
    hd = nharm // sectors
    mixer = mixing[0]
    sign = (1 - 2 * side_id).astype(jnp.float32)
    step = rotor_step[0]
    points = sector_id * phd + jnp.arange(phd, dtype=jnp.int32)
    flat = local.reshape(phd, comp * axd)
    rows = jnp.arange(2 * hd * lax.axis_size("sector"), dtype=jnp.int32)
    owner = rows // (2 * hd)
    part = rows // hd % 2
    harm = owner * hd + rows % hd
    angle = phase_angles(harm, points, nphi)
    table = jnp.where(part[:, None] == 0, jnp.cos(angle), -jnp.sin(angle))
    owned = lax.psum_scatter(matmul(table, flat), "sector", scatter_dimension=0, tiled=True)
    spectrum = owned.reshape(2, hd, comp, axd)
    coupled = couple(spectrum, sector_id * hd, gap_gain, step, sign, nphi)
    chans = coupled.shape[2]
    piece = lax.all_gather(coupled, "sector", axis=1, tiled=True)
    count = piece.shape[1]
    harm = jnp.arange(count, dtype=jnp.int32)
    cos_t, sin_t = inverse_terms(points, harm, nphi)
    carry = matmul(cos_t, piece[0].reshape(count, chans * axd))
    wave = carry + matmul(sin_t, piece[1].reshape(count, chans * axd))
    wave = wave.reshape(phd, chans, axd)
    source = jnp.einsum("ck,nka->cna", mixer, wave, precision=HIGH)
    rhs = current[0].at[:, 0].add(source)
    diag_part = cond_diag[0]
    off_part = cond_off[0]
    da = 6.0 + diag_part[0]
    db = 6.0 + diag_part[1]
    dc = 6.0 + diag_part[2]
    op, oq, orr = (off_part[0], off_part[1], off_part[2])
    c00 = db * dc - orr * orr
    c01 = oq * orr - op * dc
    c02 = op * orr - oq * db
    c11 = da * dc - oq * oq
    c12 = op * oq - da * orr
    c22 = da * db - op * op
    inv_det = 1.0 / (da * c00 + op * c01 + oq * c02)
    potential = field[0]
    for sweep in range(SWEEPS):
        beside_all = extended(potential, (("sector", 2),), 1, True)
        axial = extended(potential, (("slab", 3),), 1, False)
        radial = jnp.pad(potential, ((0, 0), (1, 1), (0, 0), (0, 0)))
        beside = radial[:, 2:] + radial[:, :-2]
        beside = beside + beside_all[:, :, 2:] + beside_all[:, :, :-2]
        beside = beside + axial[..., 2:] + axial[..., :-2]
        y = rhs + beside
        x0 = (c00 * y[0] + c01 * y[1] + c02 * y[2]) * inv_det
        x1 = (c01 * y[0] + c11 * y[1] + c12 * y[2]) * inv_det
        x2 = (c02 * y[0] + c12 * y[1] + c22 * y[2]) * inv_det
        potential = jnp.stack([x0, x1, x2])
    return potential[None]


def solution(mesh):
    placed = (
        P("side", "sector", None, "slab"),
        P(),
        P(),
        P("side", None, None),
        P("side", None, None, "sector", "slab"),
        P("side", None, None, "sector", "slab"),
        P("side", None, None, "sector", "slab"),
        P("side", None, None, "sector", "slab"),
    )
    return jax.shard_map(
        shards,
        mesh=mesh,
        in_specs=placed,
        out_specs=P("side", None, None, "sector", "slab"),
        check_vma=False,
    )
```

profile of v0, /device:TPU:1, one launch (start us, length us, event | category | flops | bytes accessed | tf_op | source)
XLA Modules:
  0.0 611.7 jit_solution(11923855958361879836)
XLA Ops:
  7.6 14.1 %fusion.17 = f32[2048,1024]{1,0:T(8,128)} fusion(f32[64,1024]{1,0:T(8,128)S(1)} %bitcast.148, s32[64]{0:T(128)S(1)} %iota_add_fusion, s32[2048]{0:T(1024)S(1)} %fusion.62, pred[2048]{0:T(1024)(128)(4,1)S(1)} %fusion.59), kind=kOutput, calls=%fused_computation.48 | convolution fusion | flops 1612709888 | bytes 8661248 | tf_op jit(solution)/shard_map/dot_general | solution.py:47
  22.6 336.7 %reduce-scatter.2.cloned.1.call-done = f32[32,1024]{1,0:T(8,128)} async-done(((f32[2048,1024]{1,0:T(8,128)}), f32[32,1024]{1,0:T(8,128)}) %reduce-scatter.2.cloned.1.call-update) | async-done | bytes 131088 | tf_op jit(solution)/shard_map/reduce_scatter | solution.py:89
  360.4 46.7 %collective-permute-start = (f32[2,16,4,256]{3,2,1,0:T(4,128)S(1)}, f32[2,16,4,256]{3,2,1,0:T(4,128)S(1)}, u32[]{:S(2)}, u32[]{:S(2)}) collective-permute-start(f32[2,16,4,256]{3,2,1,0:T(4,128)S(1)} %pad_maximum_fusion.17), channel_id=1, source_target_pairs={{0,1},{1,0},{2,3},{3,2},{4,5},{5,4},{6,7},{7,6},{8,9},{9,8},{10,11... | collective-permute-start | bytes 393224 | tf_op jit(solution)/shard_map/ppermute | solution.py:21
  411.1 1.3 collective-permute-start.3
  412.7 4.0 collective-permute-start.4
  418.3 3.5 fusion.86
  425.2 124.1 %all-gather.2.cloned.1.call-done = f32[2,1024,4,256]{3,2,1,0:T(4,128)} async-done(((f32[2,16,4,256]{3,2,1,0:T(4,128)}), f32[2,1024,4,256]{3,2,1,0:T(4,128)}) %all-gather.2.cloned.1.call-update) | async-done | bytes 8388624 | tf_op jit(solution)/shard_map/all_gather | solution.py:93
  549.2 4.9 fusion.83
  556.2 3.6 fusion.42
  559.8 4.3 convolution_add_fusion
  564.2 1.8 reshape.481
  565.9 1.8 fusion.13
  568.0 2.7 scatter-add.4
  570.8 2.6 fusion.5
  573.4 2.7 add_multiply_fusion.5
  576.2 1.7 add_multiply_fusion.4
  579.9 3.8 collective-permute-start.5
  583.6 1.4 fusion.85
  585.0 1.4 copy.36
  587.7 1.4 copy.38
  589.2 4.2 collective-permute-start.8
  596.0 5.2 fusion.11
  601.3 1.9 add_multiply_fusion.1
  603.3 1.6 copy.40
  (102 shorter events, 19.5 us)
Async XLA Ops:
  6.5 352.7 %reduce-scatter.2.cloned.1.call-start = ((), (), s32[]{:S(2)}) async-start(), calls=%async_computation.1 | async-start | bytes 8519680 | tf_op jit(solution)/shard_map/reduce_scatter | solution.py:89
  21.7 387.9 %copy-start.24 = (f32[1,3,8,64,256]{4,3,2,1,0:T(8,128)S(1)}, f32[1,3,8,64,256]{4,3,2,1,0:T(8,128)}, u32[]{:S(2)}) copy-start(f32[1,3,8,64,256]{4,3,2,1,0:T(8,128)} %param.14) | copy-start | bytes 4718596
  21.7 527.5 %all-gather.2.cloned.1.call-start = ((), (), s32[]{:S(2)}) async-start(), calls=%async_computation.2 | async-start | bytes 8519680 | tf_op jit(solution)/shard_map/all_gather | solution.py:93
  360.4 48.5 %collective-permute-start = (f32[2,16,4,256]{3,2,1,0:T(4,128)S(1)}, f32[2,16,4,256]{3,2,1,0:T(4,128)S(1)}, u32[]{:S(2)}, u32[]{:S(2)}) collective-permute-start(f32[2,16,4,256]{3,2,1,0:T(4,128)S(1)} %pad_maximum_fusion.17), channel_id=1, source_target_pairs={{0,1},{1,0},{2,3},{3,2},{4,5},{5,4},{6,7},{7,6},{8,9},{9,8},{10,11... | collective-permute-start | bytes 393224 | tf_op jit(solution)/shard_map/ppermute | solution.py:21
  411.1 11.6 %collective-permute-start.3 = (f32[3,8,64,1]{2,1,3,0:T(8,128)S(1)}, f32[3,8,64,1]{2,1,3,0:T(8,128)S(1)}, u32[]{:S(2)}, u32[]{:S(2)}) collective-permute-start(f32[3,8,64,1]{2,1,3,0:T(8,128)S(1)} %copy.29), channel_id=1, source_target_pairs={{128,0},{129,1},{130,2},{131,3},{132,4},{133,5},{134,6},{135,7},{1... | collective-permute-start | bytes 18440 | tf_op jit(solution)/shard_map/ppermute | solution.py:34
  412.7 11.2 %collective-permute-start.4 = (f32[3,8,64,1]{2,1,3,0:T(8,128)S(1)}, f32[3,8,64,1]{2,1,3,0:T(8,128)S(1)}, u32[]{:S(2)}, u32[]{:S(2)}) collective-permute-start(f32[3,8,64,1]{2,1,3,0:T(8,128)S(1)} %copy.31), channel_id=1, source_target_pairs={{0,128},{1,129},{2,130},{3,131},{4,132},{5,133},{6,134},{7,135},{8... | collective-permute-start | bytes 18440 | tf_op jit(solution)/shard_map/ppermute | solution.py:32
  416.7 154.0 %collective-permute-start.1 = (f32[3,8,1,256]{3,1,2,0:T(8,128)S(1)}, f32[3,8,1,256]{3,1,2,0:T(8,128)S(1)}, u32[]{:S(2)}, u32[]{:S(2)}) collective-permute-start(f32[3,8,1,256]{3,1,2,0:T(8,128)S(1)} %get-tuple-element.39), channel_id=1, source_target_pairs={{2,0},{4,2},{6,4},{8,6},{10,8},{12,10},{14,12},{16,14},{18,16},{20... | collective-permute-start | bytes 73736 | tf_op jit(solution)/shard_map/ppermute | solution.py:34
  417.3 153.4 %collective-permute-start.2 = (f32[3,8,1,256]{3,1,2,0:T(8,128)S(1)}, f32[3,8,1,256]{3,1,2,0:T(8,128)S(1)}, u32[]{:S(2)}, u32[]{:S(2)}) collective-permute-start(f32[3,8,1,256]{3,1,2,0:T(8,128)S(1)} %get-tuple-element.40), channel_id=1, source_target_pairs={{0,2},{2,4},{4,6},{6,8},{8,10},{10,12},{12,14},{14,16},{16,18},{18... | collective-permute-start | bytes 73736 | tf_op jit(solution)/shard_map/ppermute | solution.py:32
  559.8 6.1 %slice-start = ((f32[1,3,8,64,256]{4,3,2,1,0:T(8,128)}), f32[1,3,1,64,256]{4,3,2,1,0:T(8,128)S(1)}, s32[]{:S(2)}) async-start(f32[1,3,8,64,256]{4,3,2,1,0:T(8,128)} %param.15), calls=%async_computation.3 | async-start | bytes 393216 | tf_op jit(solution)/shard_map/slice.40
  559.8 6.1 %copy-start.25 = (f32[1,3,4]{2,0,1:T(1,128)S(1)}, f32[1,3,4]{2,0,1:T(1,128)}, u32[]{:S(2)}) copy-start(f32[1,3,4]{2,0,1:T(1,128)} %param.13) | copy-start | bytes 148
  577.9 7.1 %copy-start.20 = (f32[1,8,64,256]{3,1,2,0:T(8,128)}, f32[1,8,64,256]{3,1,2,0:T(8,128)S(1)}, u32[]{:S(2)}) copy-start(f32[1,8,64,256]{3,1,2,0:T(8,128)S(1)} %get-tuple-element.22) | copy-start | bytes 1572868
  579.9 16.1 %collective-permute-start.5 = (f32[3,8,1,256]{3,1,2,0:T(8,128)S(1)}, f32[3,8,1,256]{3,1,2,0:T(8,128)S(1)}, u32[]{:S(2)}, u32[]{:S(2)}) collective-permute-start(f32[3,8,1,256]{3,1,2,0:T(8,128)S(1)} %get-tuple-element.29), channel_id=1, source_target_pairs={{2,0},{4,2},{6,4},{8,6},{10,8},{12,10},{14,12},{16,14},{18,16},{20... | collective-permute-start | bytes 73736 | tf_op jit(solution)/shard_map/ppermute | solution.py:34
  583.6 12.3 %collective-permute-start.6 = (f32[3,8,1,256]{3,1,2,0:T(8,128)S(1)}, f32[3,8,1,256]{3,1,2,0:T(8,128)S(1)}, u32[]{:S(2)}, u32[]{:S(2)}) collective-permute-start(f32[3,8,1,256]{3,1,2,0:T(8,128)S(1)} %get-tuple-element.30), channel_id=1, source_target_pairs={{0,2},{2,4},{4,6},{6,8},{8,10},{10,12},{12,14},{14,16},{16,18},{18... | collective-permute-start | bytes 73736 | tf_op jit(solution)/shard_map/ppermute | solution.py:32
  586.4 7.0 %collective-permute-start.7 = (f32[3,8,64,1]{2,1,3,0:T(8,128)S(1)}, f32[3,8,64,1]{2,1,3,0:T(8,128)S(1)}, u32[]{:S(2)}, u32[]{:S(2)}) collective-permute-start(f32[3,8,64,1]{2,1,3,0:T(8,128)S(1)} %copy.36), channel_id=1, source_target_pairs={{128,0},{129,1},{130,2},{131,3},{132,4},{133,5},{134,6},{135,7},{1... | collective-permute-start | bytes 18440 | tf_op jit(solution)/shard_map/ppermute | solution.py:34
  589.2 5.5 collective-permute-start.8
  595.9 5.3 copy-start.3
  595.9 5.3 copy-start.5
  595.9 5.3 copy-start.7
  595.9 5.3 copy-start.9
  595.9 5.3 copy-start.11
  595.9 5.3 copy-start.13
  595.9 5.3 copy-start.15
  595.9 5.3 copy-start.18
  595.9 5.3 copy-start.22
  (14 other events, 35.9 us)
Sparse Core Ops, SparseCore 0:
  21.8 337.3 reduce-scatter.1
  409.7 139.4 all-gather.1
where the time goes:
time: 616 us; the launch traced here: 612 us
  waiting for transfers between devices  461 us (75%)
  starting transfers between devices  62.9 us (10%)
  local copies, waits for them, and re-layouts  33 us (5%)
  matrix products  23.9 us (4%)
  other arithmetic  16.4 us (3%)
  between operations  14.8 us (2%)
    reduce_scatter x1, waiting for transfers between devices, shards(): lax.psum_scatter(matmul(table, flat), 'sector', scatter_dimension=0, tile...  337 us
    all_gather x1, waiting for transfers between devices, shards(): piece = lax.all_gather(coupled, 'sector', axis=1, tiled=True)  124 us
    ppermute x1, starting transfers between devices, partner(): return lax.ppermute(block, axis, route)  46.7 us
    dot_general x3, matrix products, matmul(): jnp.dot(left, right, precision=HIGH, preferred_element_type=jnp.float32)  22.1 us
  transfers between devices with their start and end apart: 11, of which 2 were waited for; matrix products, arithmetic and copies ran while one was open for 6% of the time, Pallas kernels for 0%

commit v1 on v0

v1 whole, which is shorter than its diff:
```python
import math

import jax
import jax.numpy as jnp
import ml_dtypes
import numpy as np
from jax import lax
from jax.experimental import pallas as pl
from jax.experimental.pallas import tpu as pltpu
from jax.sharding import PartitionSpec as P

SWEEPS = 2
MESH = pl.DeviceIdType.MESH
SECTORS = 64
PHD = 64
NPHI = 4096
M1 = 16
LAYERS = 8
AXD = 256
F32 = jnp.float32
BF16 = jnp.bfloat16


def split_table(table):
    high = table.astype(np.float32).astype(ml_dtypes.bfloat16)
    low = (table - high.astype(np.float64)).astype(np.float32).astype(ml_dtypes.bfloat16)
    return np.stack([high, low])


def tables():
    s = np.arange(SECTORS)
    m0 = np.arange(64)
    p = np.arange(PHD)
    m1 = np.arange(M1)
    a = 2.0 * np.pi * ((m0[:, None] * s[None, :]) % 64) / 64.0
    outer = np.concatenate([np.cos(a), -np.sin(a)], axis=0)
    b = 2.0 * np.pi * (m0[:, None] * p[None, :]) / NPHI
    twiddle = np.stack([np.tile(np.cos(b), (1, 2)), np.tile(np.sin(b), (1, 2))]).astype(np.float32)
    c = 2.0 * np.pi * ((p[:, None] * m1[None, :]) % 64) / 64.0
    groups = np.eye(8)
    cos_b = np.kron(groups, np.cos(c))
    sin_b = np.kron(groups, np.sin(c))
    inner = np.block([[cos_b, -sin_b], [sin_b, cos_b]])
    pick = np.zeros((3 * 128, 128))
    for k in range(3):
        for qa in range(2):
            pick[k * 128 + qa * 64 + 63, qa * 4 + k] = 1.0
            pick[k * 128 + qa * 64, 8 + qa * 4 + k] = 1.0
    return (
        split_table(outer),
        split_table(np.ascontiguousarray(outer.T)),
        split_table(inner),
        split_table(np.ascontiguousarray(inner.T)),
        twiddle,
        pick.astype(ml_dtypes.bfloat16),
    )


def halves(x):
    high = x.astype(BF16)
    return high, (x - high.astype(F32)).astype(BF16)


def mm(a, b):
    return jnp.dot(a, b, preferred_element_type=F32)


def dot_right(x, table):
    rows = x.shape[0]
    high, low = halves(x)
    both = mm(jnp.concatenate([high, low], axis=0), table[0])
    return both[:rows] + both[rows:] + mm(high, table[1])


def dot_left(table, x):
    high, low = halves(x)
    return mm(table[0], high) + mm(table[0], low) + mm(table[1], high)


def kernel(
    step_ref, mix_ref, gain_ref, traces_hbm, field_hbm, current_hbm, diag_hbm, off_hbm,
    f1_hbm, f2_hbm, g_hbm, h_hbm, tw_hbm, pick_hbm,
    out_hbm,
    traces, field, current, diag, off, f1, f2, g, h, tw, pick,
    dinv, a1, result, wsend, rrecv, usend, urecv, spec, other, etab,
    row_s, row_r, col_s, col_r, row2_s, row2_r, col2_s, col2_r, xcol,
    load, fsend, frecv, usem, ursem, ssend, srecv, hsend, hrecv, h2send, h2recv, xsem, osem,
):
    slab = lax.axis_index("slab")
    me = lax.axis_index("sector")
    side = lax.axis_index("side")
    nxt = lax.rem(me + 1, SECTORS)
    prv = lax.rem(me + SECTORS - 1, SECTORS)

    loads = [
        pltpu.make_async_copy(traces_hbm, traces, load.at[0]),
        pltpu.make_async_copy(field_hbm, field.at[:, pl.ds(1, LAYERS)], load.at[1]),
        pltpu.make_async_copy(diag_hbm, diag, load.at[2]),
        pltpu.make_async_copy(off_hbm, off, load.at[3]),
        pltpu.make_async_copy(current_hbm, current, load.at[4]),
        pltpu.make_async_copy(f1_hbm, f1, load.at[5]),
        pltpu.make_async_copy(f2_hbm, f2, load.at[6]),
        pltpu.make_async_copy(g_hbm, g, load.at[7]),
        pltpu.make_async_copy(h_hbm, h, load.at[8]),
        pltpu.make_async_copy(tw_hbm, tw, load.at[9]),
        pltpu.make_async_copy(pick_hbm, pick, load.at[10]),
    ]
    for copy in loads:
        copy.start()

    barrier = pltpu.get_barrier_semaphore()

    def greet(k, carry):
        pl.semaphore_signal(barrier, inc=1, device_id={"sector": lax.rem(me + k, SECTORS)}, device_id_type=MESH)
        return carry

    pl.semaphore_signal(barrier, inc=1, device_id={"side": 1 - side}, device_id_type=MESH)
    pl.semaphore_signal(barrier, inc=1, device_id={"slab": 1 - slab}, device_id_type=MESH)
    lax.fori_loop(1, SECTORS, greet, 0)

    loads[0].wait()
    for cl in range(2):
        stacked = jnp.concatenate([traces[:, cl, :], traces[:, 2 + cl, :]], axis=0)
        for qa in range(2):
            turned = stacked[:, qa * 128:(qa + 1) * 128].T
            for qb in range(2):
                wsend[pl.ds(cl * 4 + qa * 2 + qb, 64, stride=8), :] = turned[qb * 64:(qb + 1) * 64]

    pl.semaphore_wait(barrier, SECTORS + 1)

    def tile(ref, j):
        return ref.at[pl.ds(pl.multiple_of(j * 8, 8), 8)]

    own = pltpu.make_async_copy(tile(wsend, me), tile(rrecv, me), frecv)
    own.start()

    def scatter(k, carry):
        j = lax.rem(me + k, SECTORS)
        pltpu.make_async_remote_copy(
            src_ref=tile(wsend, j), dst_ref=tile(rrecv, me), send_sem=fsend, recv_sem=frecv,
            device_id={"sector": j}, device_id_type=MESH,
        ).start()
        return carry

    lax.fori_loop(1, SECTORS, scatter, 0)

    lane = lax.broadcasted_iota(jnp.int32, (64, 128), 1)
    wide = lax.broadcasted_iota(jnp.int32, (64, AXD), 1)
    high = lax.broadcasted_iota(jnp.int32, (64, AXD), 0)
    first_slab = slab == 0

    def edge_column(x):
        return jnp.where(first_slab, x[:, AXD - 1:AXD], x[:, 0:1])

    loads[1].wait()
    field[:, 0] = jnp.zeros((3, 64, AXD), F32)
    field[:, LAYERS + 1] = jnp.zeros((3, 64, AXD), F32)
    a1[:, 0] = jnp.zeros((3, 64, AXD), F32)
    a1[:, LAYERS + 1] = jnp.zeros((3, 64, AXD), F32)

    def edges(k, carry):
        columns = col_s[...]
        for c in range(3):
            x = field[c, k + 1]
            row_s[0, pl.ds(c * 8 + k, 1), :] = x[63:64]
            row_s[1, pl.ds(c * 8 + k, 1), :] = x[0:1]
            columns = jnp.where(lane == c * 8 + k, edge_column(x), columns)
        col_s[...] = columns
        return carry

    lax.fori_loop(0, LAYERS, edges, 0)

    def halo(rows_s, rows_r, cols_s, cols_r, send, recv):
        return [
            pltpu.make_async_remote_copy(
                src_ref=rows_s.at[0], dst_ref=rows_r.at[0], send_sem=send.at[0], recv_sem=recv.at[0],
                device_id={"sector": nxt}, device_id_type=MESH,
            ),
            pltpu.make_async_remote_copy(
                src_ref=rows_s.at[1], dst_ref=rows_r.at[1], send_sem=send.at[1], recv_sem=recv.at[1],
                device_id={"sector": prv}, device_id_type=MESH,
            ),
            pltpu.make_async_remote_copy(
                src_ref=cols_s, dst_ref=cols_r, send_sem=send.at[2], recv_sem=recv.at[2],
                device_id={"slab": 1 - slab}, device_id_type=MESH,
            ),
        ]

    halo1 = halo(row_s, row_r, col_s, col_r, hsend, hrecv)
    for copy in halo1:
        copy.start()

    loads[2].wait()
    loads[3].wait()

    def invert(k, carry):
        da = 6.0 + diag[0, k]
        db = 6.0 + diag[1, k]
        dc = 6.0 + diag[2, k]
        op, oq, orr = off[0, k], off[1, k], off[2, k]
        c00 = db * dc - orr * orr
        c01 = oq * orr - op * dc
        c02 = op * orr - oq * db
        c11 = da * dc - oq * oq
        c12 = op * oq - da * orr
        c22 = da * db - op * op
        inv = 1.0 / (da * c00 + op * c01 + oq * c02)
        for i, cof in enumerate((c00, c01, c02, c11, c12, c22)):
            dinv[i, k] = cof * inv
        return carry

    lax.fori_loop(0, LAYERS, invert, 0)

    def solve(k, y):
        d = [dinv[i, k] for i in range(6)]
        return (
            d[0] * y[0] + d[1] * y[1] + d[2] * y[2],
            d[1] * y[0] + d[3] * y[1] + d[4] * y[2],
            d[2] * y[0] + d[4] * y[1] + d[5] * y[2],
        )

    def beside(x, prev_row, next_row, column):
        up = jnp.where(high == 0, prev_row, pltpu.roll(x, 1, 0))
        down = jnp.where(high == 63, next_row, pltpu.roll(x, 63, 0))
        left = jnp.where(wide == 0, jnp.where(first_slab, 0.0, column), pltpu.roll(x, 1, 1))
        right = jnp.where(wide == AXD - 1, jnp.where(first_slab, column, 0.0), pltpu.roll(x, AXD - 1, 1))
        return up + down + (left + right)

    def relax(k, src, rows_r, cols_r):
        y = []
        for c in range(3):
            x = src[c, k + 1]
            column = pltpu.roll(cols_r[...], 128 - c * 8 - k, 1)[:, 0:1]
            near = beside(x, rows_r[0, pl.ds(c * 8 + k, 1), :], rows_r[1, pl.ds(c * 8 + k, 1), :], column)
            y.append(current[c, k] + (src[c, k] + src[c, k + 2] + near))
        return solve(k, y)

    for copy in halo1:
        copy.wait_recv()
    loads[4].wait()

    def sweep1(k, carry):
        new = relax(k, field, row_r, col_r)
        columns = col2_s[...]
        for c in range(3):
            a1[c, k + 1] = new[c]
            row2_s[0, pl.ds(c * 8 + k, 1), :] = new[c][63:64]
            row2_s[1, pl.ds(c * 8 + k, 1), :] = new[c][0:1]
            columns = jnp.where(lane == c * 8 + k, edge_column(new[c]), columns)
        col2_s[...] = columns
        return carry

    lax.fori_loop(0, LAYERS, sweep1, 0)
    columns = col2_s[...]
    for i in range(6):
        x = dinv[i, 0]
        row2_s[0, 24 + i:25 + i, :] = x[63:64]
        row2_s[1, 24 + i:25 + i, :] = x[0:1]
        columns = jnp.where(lane == 24 + i, edge_column(x), columns)
    col2_s[...] = columns
    halo2 = halo(row2_s, row2_r, col2_s, col2_r, h2send, h2recv)
    for copy in halo2:
        copy.start()

    m1 = lane % M1
    harm = lax.broadcasted_iota(jnp.int32, (64, 128), 0) + 64 * m1
    angle = (harm * step_ref[0] % NPHI).astype(F32) * (2.0 * math.pi / NPHI)
    weight = jnp.where(harm == 0, 1.0 / NPHI, 2.0 / NPHI)
    turned = gain_ref[...].T
    gain = jnp.zeros((64, 128), F32)
    for i in range(8):
        gain = jnp.where(m1 == 2 * i, turned[:64, i:i + 1], gain)
        gain = jnp.where(m1 == 2 * i + 1, turned[64:, i:i + 1], gain)
    scaled = gain * weight
    sign = (2 * side - 1).astype(F32)
    etab[0] = weight
    etab[1] = scaled * jnp.cos(angle)
    etab[2] = scaled * jnp.sin(angle) * sign

    for copy in loads[5:]:
        copy.wait()
    pltpu.make_async_copy(wsend, rrecv, frecv).wait()

    exchange = []
    for qb in range(2):
        x = jnp.concatenate([rrecv[pl.ds(2 * r + qb, 64, stride=8), :] for r in range(4)], axis=1)
        y = dot_left(f1, x)
        cos_t = jnp.concatenate([tw[0]] * 4, axis=1)
        sin_t = jnp.concatenate([tw[1]] * 4, axis=1)
        re, im = y[:64], y[64:]
        t = jnp.concatenate([re * cos_t + im * sin_t, im * cos_t - re * sin_t], axis=1)
        spec[qb] = dot_right(t, g)
        copy = pltpu.make_async_remote_copy(
            src_ref=spec.at[qb], dst_ref=other.at[qb], send_sem=ssend.at[qb], recv_sem=srecv.at[qb],
            device_id={"side": 1 - side}, device_id_type=MESH,
        )
        copy.start()
        exchange.append(copy)

    left_half = lane < 64
    for qb in range(2):
        exchange[qb].wait_recv()
        sre, sim = spec[qb, :, :128], spec[qb, :, 128:]
        ore, oim = other[qb, :, :128], other[qb, :, 128:]
        w, ec, es = etab[0], etab[1], etab[2]
        c = jnp.concatenate([w * sre + ec * ore - es * oim, w * sim + ec * oim + es * ore], axis=1)
        z = dot_right(c, h)
        re, im = z[:, :512], z[:, 512:]
        cos_t = jnp.concatenate([tw[0]] * 4, axis=1)
        sin_t = jnp.concatenate([tw[1]] * 4, axis=1)
        x = dot_left(f2, jnp.concatenate([re * cos_t - im * sin_t, im * cos_t + re * sin_t], axis=0))
        packed = []
        for k in range(3):
            coef = [jnp.where(left_half, mix_ref[k, cl], mix_ref[k, 2 + cl]) for cl in range(2)]
            mixed = []
            for qa in range(2):
                v = coef[0] * x[:, qa * 128:(qa + 1) * 128] + coef[1] * x[:, (2 + qa) * 128:(3 + qa) * 128]
                mixed.append(v + pltpu.roll(v, 64, 1))
            packed.append(jnp.where(left_half, mixed[0], mixed[1]))
            usend[pl.ds(2 * k + qb, 64, stride=8), :] = packed[k]
        ph, plow = halves(jnp.concatenate(packed, axis=1))
        ends = mm(ph, pick[...]) + mm(plow, pick[...])
        usend[pl.ds(6 + qb, 64, stride=8), :] = jnp.where(lane < 8, pltpu.roll(ends, 1, 0), pltpu.roll(ends, 63, 0))

    special = jnp.where(first_slab, SECTORS - 1, 0)
    mine = jnp.where(me == special, 1, 0)
    pltpu.make_async_copy(tile(usend, me), tile(urecv, me), ursem.at[mine]).start()

    def gather(k, carry):
        j = lax.rem(me + k, SECTORS)
        pltpu.make_async_remote_copy(
            src_ref=tile(usend, j), dst_ref=tile(urecv, me), send_sem=usem, recv_sem=ursem.at[mine],
            device_id={"sector": j}, device_id_type=MESH,
        ).start()
        return carry

    lax.fori_loop(1, SECTORS, gather, 0)

    for copy in halo2:
        copy.wait_recv()

    def sweep2(k, carry):
        new = relax(k, a1, row2_r, col2_r)
        for c in range(3):
            result[c, k] = new[c]
        return carry

    lax.fori_loop(0, LAYERS, sweep2, 0)
    outs = [pltpu.make_async_copy(result.at[:, pl.ds(2, 6)], out_hbm.at[:, pl.ds(2, 6)], osem.at[0])]
    outs[0].start()

    pltpu.make_async_copy(tile(usend, 0), tile(urecv, 0), ursem.at[1]).wait()
    forward = pltpu.make_async_remote_copy(
        src_ref=tile(urecv, special), dst_ref=xcol, send_sem=xsem.at[0], recv_sem=xsem.at[1],
        device_id={"slab": 1 - slab}, device_id_type=MESH,
    )
    forward.start()
    pltpu.make_async_copy(usend.at[pl.ds(0, 504)], urecv.at[pl.ds(0, 504)], ursem.at[0]).wait()

    turned = []
    for k in range(4):
        both = jnp.concatenate([urecv[pl.ds(2 * k + qb, 64, stride=8), :] for qb in range(2)], axis=0)
        turned.append(both.T)
    source = [jnp.concatenate([turned[c][:64], turned[c][64:]], axis=1) for c in range(3)]
    src_prev = [jnp.concatenate([turned[3][c:c + 1], turned[3][4 + c:5 + c]], axis=1) for c in range(3)]
    src_next = [jnp.concatenate([turned[3][8 + c:9 + c], turned[3][12 + c:13 + c]], axis=1) for c in range(3)]
    delta = solve(0, source)

    def apply(d, y):
        return (
            d[0] * y[0] + d[1] * y[1] + d[2] * y[2],
            d[1] * y[0] + d[3] * y[1] + d[4] * y[2],
            d[2] * y[0] + d[4] * y[1] + d[5] * y[2],
        )

    delta_prev = apply([row2_r[0, 24 + i:25 + i, :] for i in range(6)], src_prev)
    delta_next = apply([row2_r[1, 24 + i:25 + i, :] for i in range(6)], src_next)
    forward.wait_recv()
    cols = xcol[...].T
    cols = [jnp.where(first_slab, cols[:64, 2 * c:2 * c + 1], cols[64:, 2 * c + 1:2 * c + 2]) for c in range(3)]
    dcol = col2_r[...]
    delta_col = apply([dcol[:, 24 + i:25 + i] for i in range(6)], cols)
    y = [source[c] + beside(delta[c], delta_prev[c], delta_next[c], delta_col[c]) for c in range(3)]
    low = solve(0, y)
    up = solve(1, delta)
    for c in range(3):
        result[c, 0] = result[c, 0] + low[c]
        result[c, 1] = result[c, 1] + up[c]
    outs.append(pltpu.make_async_copy(result.at[:, pl.ds(0, 2)], out_hbm.at[:, pl.ds(0, 2)], osem.at[1]))
    outs[1].start()

    pltpu.make_async_copy(wsend.at[pl.ds(0, 504)], rrecv.at[pl.ds(0, 504)], fsend).wait()
    pltpu.make_async_copy(usend.at[pl.ds(0, 504)], urecv.at[pl.ds(0, 504)], usem).wait()
    for copy in halo1 + halo2 + exchange + [forward]:
        copy.wait_send()
    for copy in outs:
        copy.wait()


def shards(traces, gap_gain, rotor_step, mixing, field, current, cond_diag, cond_off):
    consts = [jnp.asarray(t) for t in tables()]
    hbm = pl.BlockSpec(memory_space=pl.ANY)
    smem = pl.BlockSpec(memory_space=pltpu.SMEM)
    vmem = pl.BlockSpec(memory_space=pltpu.VMEM)
    block = (3, LAYERS, PHD, AXD)
    dma = pltpu.SemaphoreType.DMA
    v = pltpu.VMEM
    out = pl.pallas_call(
        kernel,
        out_shape=jax.ShapeDtypeStruct(block, F32),
        in_specs=[smem, smem, vmem] + [hbm] * 11,
        out_specs=hbm,
        scratch_shapes=[
            v((64, 4, AXD), F32), v((3, LAYERS + 2, 64, AXD), F32), v(block, F32), v(block, F32), v(block, F32),
            v((2, 128, 64), BF16), v((2, 64, 128), BF16), v((2, 1024, 256), BF16), v((2, 256, 1024), BF16),
            v((2, 64, 128), F32), v((384, 128), BF16),
            v((6, LAYERS, 64, AXD), F32), v((3, LAYERS + 2, 64, AXD), F32), v(block, F32),
            v((512, 128), F32), v((512, 128), F32), v((512, 128), F32), v((512, 128), F32),
            v((2, 64, 256), F32), v((2, 64, 256), F32), v((3, 64, 128), F32),
            v((2, 24, AXD), F32), v((2, 24, AXD), F32), v((64, 128), F32), v((64, 128), F32),
            v((2, 32, AXD), F32), v((2, 32, AXD), F32), v((64, 128), F32), v((64, 128), F32),
            v((8, 128), F32),
            dma((11,)), dma, dma, dma, dma((2,)), dma((2,)), dma((2,)),
            dma((3,)), dma((3,)), dma((3,)), dma((3,)), dma((2,)), dma((2,)),
        ],
        compiler_params=pltpu.CompilerParams(collective_id=0, has_side_effects=True, vmem_limit_bytes=40 * 1024 * 1024),
        cost_estimate=pl.CostEstimate(flops=400_000_000, bytes_accessed=10_000_000, transcendentals=0),
    )(
        rotor_step, mixing[0], gap_gain.reshape(8, 128), traces[0], field[0], current[0], cond_diag[0], cond_off[0],
        *consts,
    )
    return out[None]


def solution(mesh):
    placed = (
        P("side", "sector", None, "slab"),
        P(),
        P(),
        P("side", None, None),
        P("side", None, None, "sector", "slab"),
        P("side", None, None, "sector", "slab"),
        P("side", None, None, "sector", "slab"),
        P("side", None, None, "sector", "slab"),
    )
    return jax.shard_map(
        shards,
        mesh=mesh,
        in_specs=placed,
        out_specs=P("side", None, None, "sector", "slab"),
        check_vma=False,
    )
```

time: 616 us -> 58.5 us (0.09)
  the two profiles are of different devices: /device:TPU:1 before, /device:TPU:34 now
where the time goes in v1:
time: 58.5 us; the launch traced here: 58 us
  Pallas kernels  42.5 us (73%)
  local copies, waits for them, and re-layouts  14.9 us (25%)
  between operations  0.67 us (1%)
    pallas_call x1, Pallas kernels, shards(): pl.pallas_call(kernel, out_shape=jax.ShapeDtypeStruct(block, F32), in_spe...  42.5 us
    unnamed x26, local copies, waits for them, and re-layouts  14.9 us

profile of v1, /device:TPU:34, one launch (start us, length us, event | category | flops | bytes accessed | tf_op | source)
XLA Modules:
  0.0 58.0 jit_solution(584833122005237239)
XLA Ops:
  0.7 0.7 %copy.17 = f32[1,3,4]{2,1,0:T(4,128)S(1)} copy(f32[1,3,4]{2,0,1:T(1,128)} %param.17) | data formatting | bytes 96
  1.3 0.0 copy-start
  1.3 1.4 %copy-done = f32[1,3,8,64,256]{4,3,2,1,0:T(8,128)S(1)} copy-done((f32[1,3,8,64,256]{4,3,2,1,0:T(8,128)S(1)}, f32[1,3,8,64,256]{4,3,2,1,0:T(8,128)}, u32[]{:S(2)}) %copy-start) | copy-done | bytes 1572888
  2.7 0.0 copy-start.1
  2.7 1.4 %copy-done.1 = f32[1,3,8,64,256]{4,3,2,1,0:T(8,128)S(1)} copy-done((f32[1,3,8,64,256]{4,3,2,1,0:T(8,128)S(1)}, f32[1,3,8,64,256]{4,3,2,1,0:T(8,128)}, u32[]{:S(2)}) %copy-start.1) | copy-done | bytes 1572888
  4.2 0.0 copy-start.2
  4.2 1.4 %copy-done.2 = f32[1,3,8,64,256]{4,3,2,1,0:T(8,128)S(1)} copy-done((f32[1,3,8,64,256]{4,3,2,1,0:T(8,128)S(1)}, f32[1,3,8,64,256]{4,3,2,1,0:T(8,128)}, u32[]{:S(2)}) %copy-start.2) | copy-done | bytes 1572888
  5.6 0.0 copy-start.3
  5.6 1.4 %copy-done.3 = f32[1,3,8,64,256]{4,3,2,1,0:T(8,128)S(1)} copy-done((f32[1,3,8,64,256]{4,3,2,1,0:T(8,128)S(1)}, f32[1,3,8,64,256]{4,3,2,1,0:T(8,128)}, u32[]{:S(2)}) %copy-start.3) | copy-done | bytes 1572888
  7.0 0.0 copy-start.4
  7.0 1.2 %copy-done.4 = bf16[2,256,1024]{2,1,0:T(8,128)(2,1)S(1)} copy-done((bf16[2,256,1024]{2,1,0:T(8,128)(2,1)S(1)}, bf16[2,256,1024]{2,1,0:T(8,128)(2,1)}, u32[]{:S(2)}) %copy-start.4) | copy-done | bytes 1048600
  8.2 0.0 copy-start.5
  8.2 1.2 %copy-done.5 = bf16[2,1024,256]{2,1,0:T(8,128)(2,1)S(1)} copy-done((bf16[2,1024,256]{2,1,0:T(8,128)(2,1)S(1)}, bf16[2,1024,256]{2,1,0:T(8,128)(2,1)}, u32[]{:S(2)}) %copy-start.5) | copy-done | bytes 1048600
  9.4 0.0 copy-start.6
  9.4 0.9 %copy-done.6 = f32[1,64,4,256]{3,2,1,0:T(4,128)S(1)} copy-done((f32[1,64,4,256]{3,2,1,0:T(4,128)S(1)}, f32[1,64,4,256]{3,2,1,0:T(4,128)}, u32[]{:S(2)}) %copy-start.6) | copy-done | bytes 262168
  10.4 0.0 copy-start.7
  10.4 0.9 %copy-done.7 = bf16[384,128]{1,0:T(8,128)(2,1)S(1)} copy-done((bf16[384,128]{1,0:T(8,128)(2,1)S(1)}, bf16[384,128]{1,0:T(8,128)(2,1)}, u32[]{:S(2)}) %copy-start.7) | copy-done | bytes 98328
  11.3 0.8 %copy-done.8 = f32[2,64,128]{2,1,0:T(8,128)S(1)} copy-done((f32[2,64,128]{2,1,0:T(8,128)S(1)}, f32[2,64,128]{2,1,0:T(8,128)}, u32[]{:S(2)}) %copy-start.8) | copy-done | bytes 65560
  12.1 0.8 %copy-done.9 = bf16[2,128,64]{2,1,0:T(8,128)(2,1)S(1)} copy-done((bf16[2,128,64]{2,1,0:T(8,128)(2,1)S(1)}, bf16[2,128,64]{2,1,0:T(8,128)(2,1)}, u32[]{:S(2)}) %copy-start.9) | copy-done | bytes 32792
  12.9 0.8 %copy-done.10 = bf16[2,64,128]{2,1,0:T(8,128)(2,1)S(1)} copy-done((bf16[2,64,128]{2,1,0:T(8,128)(2,1)S(1)}, bf16[2,64,128]{2,1,0:T(8,128)(2,1)}, u32[]{:S(2)}) %copy-start.10) | copy-done | bytes 32792
  13.7 0.0 copy-start.11
  13.7 0.7 %copy-done.11 = f32[1024]{0:T(1024)S(1)} copy-done((f32[1024]{0:T(1024)S(1)}, f32[1024]{0:T(1024)}, u32[]{:S(2)}) %copy-start.11) | copy-done | bytes 4120
  14.4 42.5 %shard_map.136 = f32[3,8,64,256]{3,2,1,0:T(8,128)S(1)} custom-call(s32[1]{0:T(128)S(6)} %copy.19.step_ref, f32[3,4]{1,0:T(4,128)S(1)} %bitcast.16, f32[8,128]{1,0:T(8,128)S(1)} %bitcast.17, f32[64,4,256]{2,1,0:T(4,128)S(1)} %bitcast.15, f32[3,8,64,256]{3,2,1,0:T(8,128)S(1)} %bitcast.11, f32[3,8,64,256]{3,2,1,0:T(8,128)S(1)} %bitcast.12, ...), custom_call_target="tpu_custom_call" | custom-call | flops 400000000 | bytes 10000000 | tf_op jit(solution)/shard_map/pallas_call | solution.py:408
  56.9 1.1 %copy.20 = f32[1,3,8,64,256]{4,3,2,1,0:T(8,128)} copy(f32[1,3,8,64,256]{4,3,2,1,0:T(8,128)S(1)} %bitcast.10) | data formatting | bytes 3145728
  (3 shorter events, 0.0 us)
Async XLA Ops:
  1.3 1.4 %copy-start = (f32[1,3,8,64,256]{4,3,2,1,0:T(8,128)S(1)}, f32[1,3,8,64,256]{4,3,2,1,0:T(8,128)}, u32[]{:S(2)}) copy-start(f32[1,3,8,64,256]{4,3,2,1,0:T(8,128)} %param.18) | copy-start | bytes 4718596
  2.7 1.4 %copy-start.1 = (f32[1,3,8,64,256]{4,3,2,1,0:T(8,128)S(1)}, f32[1,3,8,64,256]{4,3,2,1,0:T(8,128)}, u32[]{:S(2)}) copy-start(f32[1,3,8,64,256]{4,3,2,1,0:T(8,128)} %param.19) | copy-start | bytes 4718596
  4.2 1.4 %copy-start.2 = (f32[1,3,8,64,256]{4,3,2,1,0:T(8,128)S(1)}, f32[1,3,8,64,256]{4,3,2,1,0:T(8,128)}, u32[]{:S(2)}) copy-start(f32[1,3,8,64,256]{4,3,2,1,0:T(8,128)} %param.20) | copy-start | bytes 4718596
  5.6 1.4 %copy-start.3 = (f32[1,3,8,64,256]{4,3,2,1,0:T(8,128)S(1)}, f32[1,3,8,64,256]{4,3,2,1,0:T(8,128)}, u32[]{:S(2)}) copy-start(f32[1,3,8,64,256]{4,3,2,1,0:T(8,128)} %param.21) | copy-start | bytes 4718596
  7.0 1.2 %copy-start.4 = (bf16[2,256,1024]{2,1,0:T(8,128)(2,1)S(1)}, bf16[2,256,1024]{2,1,0:T(8,128)(2,1)}, u32[]{:S(2)}) copy-start(bf16[2,256,1024]{2,1,0:T(8,128)(2,1)} %constant.15.clone.h_hbm) | copy-start | bytes 3145732
  8.2 1.2 %copy-start.5 = (bf16[2,1024,256]{2,1,0:T(8,128)(2,1)S(1)}, bf16[2,1024,256]{2,1,0:T(8,128)(2,1)}, u32[]{:S(2)}) copy-start(bf16[2,1024,256]{2,1,0:T(8,128)(2,1)} %constant.14.clone.g_hbm) | copy-start | bytes 3145732
  9.4 0.9 %copy-start.6 = (f32[1,64,4,256]{3,2,1,0:T(4,128)S(1)}, f32[1,64,4,256]{3,2,1,0:T(4,128)}, u32[]{:S(2)}) copy-start(f32[1,64,4,256]{3,2,1,0:T(4,128)} %param.14) | copy-start | bytes 786436
  10.4 0.9 %copy-start.7 = (bf16[384,128]{1,0:T(8,128)(2,1)S(1)}, bf16[384,128]{1,0:T(8,128)(2,1)}, u32[]{:S(2)}) copy-start(bf16[384,128]{1,0:T(8,128)(2,1)} %constant.17.clone.pick_hbm) | copy-start | bytes 294916
  11.3 0.8 %copy-start.8 = (f32[2,64,128]{2,1,0:T(8,128)S(1)}, f32[2,64,128]{2,1,0:T(8,128)}, u32[]{:S(2)}) copy-start(f32[2,64,128]{2,1,0:T(8,128)} %constant.16.clone.tw_hbm) | copy-start | bytes 196612
  12.1 0.8 %copy-start.9 = (bf16[2,128,64]{2,1,0:T(8,128)(2,1)S(1)}, bf16[2,128,64]{2,1,0:T(8,128)(2,1)}, u32[]{:S(2)}) copy-start(bf16[2,128,64]{2,1,0:T(8,128)(2,1)} %constant.12.clone.f1_hbm) | copy-start | bytes 98308
  12.9 0.8 %copy-start.10 = (bf16[2,64,128]{2,1,0:T(8,128)(2,1)S(1)}, bf16[2,64,128]{2,1,0:T(8,128)(2,1)}, u32[]{:S(2)}) copy-start(bf16[2,64,128]{2,1,0:T(8,128)(2,1)} %constant.13.clone.f2_hbm) | copy-start | bytes 98308
  13.7 0.7 %copy-start.11 = (f32[1024]{0:T(1024)S(1)}, f32[1024]{0:T(1024)}, u32[]{:S(2)}) copy-start(f32[1024]{0:T(1024)} %param.15) | copy-start | bytes 12292

commit v2 on v1

--- a/solution.py
+++ b/solution.py
@@ -78,13 +78,13 @@
 
 
 def kernel(
-    step_ref, mix_ref, gain_ref, traces_hbm, field_hbm, current_hbm, diag_hbm, off_hbm,
+    step_hbm, mix_hbm, gain_hbm, traces_hbm, field_hbm, current_hbm, diag_hbm, off_hbm,
     f1_hbm, f2_hbm, g_hbm, h_hbm, tw_hbm, pick_hbm,
-    out_hbm,
-    traces, field, current, diag, off, f1, f2, g, h, tw, pick,
-    dinv, a1, result, wsend, rrecv, usend, urecv, spec, other, etab,
+    result,
+    step_ref, mix_ref, gain_ref, traces, field, current, diag, off, f1, f2, g, h, tw, pick,
+    dinv, a1, wsend, rrecv, usend, urecv, spec, other, etab,
     row_s, row_r, col_s, col_r, row2_s, row2_r, col2_s, col2_r, xcol,
-    load, fsend, frecv, usem, ursem, ssend, srecv, hsend, hrecv, h2send, h2recv, xsem, osem,
+    load, fsend, frecv, usem, ursem, ssend, srecv, hsend, hrecv, h2send, h2recv, xsem,
 ):
     slab = lax.axis_index("slab")
     me = lax.axis_index("sector")
@@ -104,19 +104,26 @@
         pltpu.make_async_copy(h_hbm, h, load.at[8]),
         pltpu.make_async_copy(tw_hbm, tw, load.at[9]),
         pltpu.make_async_copy(pick_hbm, pick, load.at[10]),
+        pltpu.make_async_copy(step_hbm, step_ref, load.at[11]),
+        pltpu.make_async_copy(mix_hbm, mix_ref, load.at[12]),
+        pltpu.make_async_copy(gain_hbm, gain_ref, load.at[13]),
     ]
     for copy in loads:
         copy.start()
 
     barrier = pltpu.get_barrier_semaphore()
 
+    def turn(k):
+        return lax.rem(me + 18 + k, SECTORS)
+
     def greet(k, carry):
-        pl.semaphore_signal(barrier, inc=1, device_id={"sector": lax.rem(me + k, SECTORS)}, device_id_type=MESH)
-        return carry
-
+        pl.semaphore_signal(barrier, inc=1, device_id={"slab": 1 - slab, "sector": turn(k)}, device_id_type=MESH)
+        return carry
+
+    lax.fori_loop(0, SECTORS, greet, 0)
     pl.semaphore_signal(barrier, inc=1, device_id={"side": 1 - side}, device_id_type=MESH)
-    pl.semaphore_signal(barrier, inc=1, device_id={"slab": 1 - slab}, device_id_type=MESH)
-    lax.fori_loop(1, SECTORS, greet, 0)
+    pl.semaphore_signal(barrier, inc=1, device_id={"sector": nxt}, device_id_type=MESH)
+    pl.semaphore_signal(barrier, inc=1, device_id={"sector": prv}, device_id_type=MESH)
 
     loads[0].wait()
     for cl in range(2):
@@ -126,23 +133,8 @@
             for qb in range(2):
                 wsend[pl.ds(cl * 4 + qa * 2 + qb, 64, stride=8), :] = turned[qb * 64:(qb + 1) * 64]
 
-    pl.semaphore_wait(barrier, SECTORS + 1)
-
     def tile(ref, j):
         return ref.at[pl.ds(pl.multiple_of(j * 8, 8), 8)]
-
-    own = pltpu.make_async_copy(tile(wsend, me), tile(rrecv, me), frecv)
-    own.start()
-
-    def scatter(k, carry):
-        j = lax.rem(me + k, SECTORS)
-        pltpu.make_async_remote_copy(
-            src_ref=tile(wsend, j), dst_ref=tile(rrecv, me), send_sem=fsend, recv_sem=frecv,
-            device_id={"sector": j}, device_id_type=MESH,
-        ).start()
-        return carry
-
-    lax.fori_loop(1, SECTORS, scatter, 0)
 
     lane = lax.broadcasted_iota(jnp.int32, (64, 128), 1)
     wide = lax.broadcasted_iota(jnp.int32, (64, AXD), 1)
@@ -186,9 +178,21 @@
             ),
         ]
 
+    pl.semaphore_wait(barrier, SECTORS + 3)
+
     halo1 = halo(row_s, row_r, col_s, col_r, hsend, hrecv)
     for copy in halo1:
         copy.start()
+
+    def scatter(k, carry):
+        j = turn(k)
+        pltpu.make_async_remote_copy(
+            src_ref=tile(wsend, j), dst_ref=tile(rrecv, me), send_sem=fsend, recv_sem=frecv,
+            device_id={"slab": 1 - slab, "sector": j}, device_id_type=MESH,
+        ).start()
+        return carry
+
+    lax.fori_loop(0, SECTORS, scatter, 0)
 
     loads[2].wait()
     loads[3].wait()
@@ -262,6 +266,9 @@
     for copy in halo2:
         copy.start()
 
+    for copy in loads[11:]:
+        copy.wait()
+
     m1 = lane % M1
     harm = lax.broadcasted_iota(jnp.int32, (64, 128), 0) + 64 * m1
     angle = (harm * step_ref[0] % NPHI).astype(F32) * (2.0 * math.pi / NPHI)
@@ -277,7 +284,7 @@
     etab[1] = scaled * jnp.cos(angle)
     etab[2] = scaled * jnp.sin(angle) * sign
 
-    for copy in loads[5:]:
+    for copy in loads[5:11]:
         copy.wait()
     pltpu.make_async_copy(wsend, rrecv, frecv).wait()
 
@@ -311,7 +318,7 @@
         x = dot_left(f2, jnp.concatenate([re * cos_t - im * sin_t, im * cos_t + re * sin_t], axis=0))
         packed = []
         for k in range(3):
-            coef = [jnp.where(left_half, mix_ref[k, cl], mix_ref[k, 2 + cl]) for cl in range(2)]
+            coef = [jnp.where(left_half, mix_ref[k, 0, cl], mix_ref[k, 0, 2 + cl]) for cl in range(2)]
             mixed = []
             for qa in range(2):
                 v = coef[0] * x[:, qa * 128:(qa + 1) * 128] + coef[1] * x[:, (2 + qa) * 128:(3 + qa) * 128]
@@ -323,18 +330,17 @@
         usend[pl.ds(6 + qb, 64, stride=8), :] = jnp.where(lane < 8, pltpu.roll(ends, 1, 0), pltpu.roll(ends, 63, 0))
 
     special = jnp.where(first_slab, SECTORS - 1, 0)
-    mine = jnp.where(me == special, 1, 0)
-    pltpu.make_async_copy(tile(usend, me), tile(urecv, me), ursem.at[mine]).start()
+    mine = jnp.where(me == SECTORS - 1 - special, 1, 0)
 
     def gather(k, carry):
-        j = lax.rem(me + k, SECTORS)
+        j = turn(k)
         pltpu.make_async_remote_copy(
             src_ref=tile(usend, j), dst_ref=tile(urecv, me), send_sem=usem, recv_sem=ursem.at[mine],
-            device_id={"sector": j}, device_id_type=MESH,
+            device_id={"slab": 1 - slab, "sector": j}, device_id_type=MESH,
         ).start()
         return carry
 
-    lax.fori_loop(1, SECTORS, gather, 0)
+    lax.fori_loop(0, SECTORS, gather, 0)
 
     for copy in halo2:
         copy.wait_recv()
@@ -346,8 +352,6 @@
         return carry
 
     lax.fori_loop(0, LAYERS, sweep2, 0)
-    outs = [pltpu.make_async_copy(result.at[:, pl.ds(2, 6)], out_hbm.at[:, pl.ds(2, 6)], osem.at[0])]
-    outs[0].start()
 
     pltpu.make_async_copy(tile(usend, 0), tile(urecv, 0), ursem.at[1]).wait()
     forward = pltpu.make_async_remote_copy(
@@ -386,21 +390,16 @@
     for c in range(3):
         result[c, 0] = result[c, 0] + low[c]
         result[c, 1] = result[c, 1] + up[c]
-    outs.append(pltpu.make_async_copy(result.at[:, pl.ds(0, 2)], out_hbm.at[:, pl.ds(0, 2)], osem.at[1]))
-    outs[1].start()
-
-    pltpu.make_async_copy(wsend.at[pl.ds(0, 504)], rrecv.at[pl.ds(0, 504)], fsend).wait()
-    pltpu.make_async_copy(usend.at[pl.ds(0, 504)], urecv.at[pl.ds(0, 504)], usem).wait()
+
+    pltpu.make_async_copy(wsend, rrecv, fsend).wait()
+    pltpu.make_async_copy(usend, urecv, usem).wait()
     for copy in halo1 + halo2 + exchange + [forward]:
         copy.wait_send()
-    for copy in outs:
-        copy.wait()
 
 
 def shards(traces, gap_gain, rotor_step, mixing, field, current, cond_diag, cond_off):
     consts = [jnp.asarray(t) for t in tables()]
-    hbm = pl.BlockSpec(memory_space=pl.ANY)
-    smem = pl.BlockSpec(memory_space=pltpu.SMEM)
+    hbm = pl.BlockSpec(memory_space=pltpu.HBM)
     vmem = pl.BlockSpec(memory_space=pltpu.VMEM)
     block = (3, LAYERS, PHD, AXD)
     dma = pltpu.SemaphoreType.DMA
@@ -408,25 +407,26 @@
     out = pl.pallas_call(
         kernel,
         out_shape=jax.ShapeDtypeStruct(block, F32),
-        in_specs=[smem, smem, vmem] + [hbm] * 11,
-        out_specs=hbm,
+        in_specs=[hbm] * 14,
+        out_specs=vmem,
         scratch_shapes=[
+            pltpu.SMEM((1,), jnp.int32), pltpu.SMEM((3, 1, 4), F32), v((8, 128), F32),
             v((64, 4, AXD), F32), v((3, LAYERS + 2, 64, AXD), F32), v(block, F32), v(block, F32), v(block, F32),
             v((2, 128, 64), BF16), v((2, 64, 128), BF16), v((2, 1024, 256), BF16), v((2, 256, 1024), BF16),
             v((2, 64, 128), F32), v((384, 128), BF16),
-            v((6, LAYERS, 64, AXD), F32), v((3, LAYERS + 2, 64, AXD), F32), v(block, F32),
+            v((6, LAYERS, 64, AXD), F32), v((3, LAYERS + 2, 64, AXD), F32),
             v((512, 128), F32), v((512, 128), F32), v((512, 128), F32), v((512, 128), F32),
             v((2, 64, 256), F32), v((2, 64, 256), F32), v((3, 64, 128), F32),
             v((2, 24, AXD), F32), v((2, 24, AXD), F32), v((64, 128), F32), v((64, 128), F32),
             v((2, 32, AXD), F32), v((2, 32, AXD), F32), v((64, 128), F32), v((64, 128), F32),
             v((8, 128), F32),
-            dma((11,)), dma, dma, dma, dma((2,)), dma((2,)), dma((2,)),
-            dma((3,)), dma((3,)), dma((3,)), dma((3,)), dma((2,)), dma((2,)),
+            dma((14,)), dma, dma, dma, dma((2,)), dma((2,)), dma((2,)),
+            dma((3,)), dma((3,)), dma((3,)), dma((3,)), dma((2,)),
         ],
-        compiler_params=pltpu.CompilerParams(collective_id=0, has_side_effects=True, vmem_limit_bytes=40 * 1024 * 1024),
+        compiler_params=pltpu.CompilerParams(collective_id=0, has_side_effects=True, vmem_limit_bytes=62 * 1024 * 1024),
         cost_estimate=pl.CostEstimate(flops=400_000_000, bytes_accessed=10_000_000, transcendentals=0),
     )(
-        rotor_step, mixing[0], gap_gain.reshape(8, 128), traces[0], field[0], current[0], cond_diag[0], cond_off[0],
+        rotor_step, jnp.transpose(mixing, (1, 0, 2)), gap_gain.reshape(8, 128), traces[0], field[0], current[0], cond_diag[0], cond_off[0],
         *consts,
     )
     return out[None]

time: 58.5 us -> 44.4 us (0.76)
  the two profiles are of different devices: /device:TPU:34 before, /device:TPU:1 now
where the time goes in v2:
time: 44.4 us; the launch traced here: 44.3 us
  Pallas kernels  40.9 us (92%)
  local copies, waits for them, and re-layouts  2.7 us (6%)
  between operations  0.66 us (1%)
    pallas_call x1, Pallas kernels, shards(): pl.pallas_call(kernel, out_shape=jax.ShapeDtypeStruct(block, F32), in_spe...  40.9 us
    unnamed x1, local copies, waits for them, and re-layouts  2.7 us

profile of v2, /device:TPU:1, one launch (start us, length us, event | category | flops | bytes accessed | tf_op | source)
XLA Modules:
  0.0 44.3 jit_solution(2441095974277118864)
XLA Ops:
  0.7 40.9 %shard_map.136 = f32[3,8,64,256]{3,2,1,0:T(8,128)} custom-call(s32[1]{0:T(128)S(6)} %copy.16.step_hbm, f32[3,1,4]{2,1,0:T(1,128)} %bitcast.15, f32[8,128]{1,0:T(8,128)} %bitcast.14, f32[64,4,256]{2,1,0:T(4,128)} %bitcast.13, f32[3,8,64,256]{3,2,1,0:T(8,128)} %bitcast.9, f32[3,8,64,256]{3,2,1,0:T(8,128)} %bitcast.10, f32[3,8,64,256]{3,2,1,0:T(8,128)} %bitcast.11, ...), custom_call_target="tpu_custom_call" | custom-call | flops 400000000 | bytes 10000000 | tf_op jit(solution)/shard_map/pallas_call | solution.py:407
  41.6 2.7 %copy.17 = f32[1,3,8,64,256]{4,3,2,1,0:T(8,128)} copy(f32[1,3,8,64,256]{4,3,2,1,0:T(8,128)} %bitcast.8) | data formatting | bytes 3145728

commit v3 on v2

--- a/solution.py
+++ b/solution.py
@@ -37,10 +37,10 @@
     b = 2.0 * np.pi * (m0[:, None] * p[None, :]) / NPHI
     twiddle = np.stack([np.tile(np.cos(b), (1, 2)), np.tile(np.sin(b), (1, 2))]).astype(np.float32)
     c = 2.0 * np.pi * ((p[:, None] * m1[None, :]) % 64) / 64.0
-    groups = np.eye(8)
-    cos_b = np.kron(groups, np.cos(c))
-    sin_b = np.kron(groups, np.sin(c))
+    cos_b = np.kron(np.eye(2), np.cos(c))
+    sin_b = np.kron(np.eye(2), np.sin(c))
     inner = np.block([[cos_b, -sin_b], [sin_b, cos_b]])
+    back = np.concatenate([inner.T, np.zeros((64, 256))], axis=0)
     pick = np.zeros((3 * 128, 128))
     for k in range(3):
         for qa in range(2):
@@ -49,8 +49,8 @@
     return (
         split_table(outer),
         split_table(np.ascontiguousarray(outer.T)),
-        split_table(inner),
-        split_table(np.ascontiguousarray(inner.T)),
+        split_table(np.tile(inner, (1, 2))),
+        split_table(back),
         twiddle,
         pick.astype(ml_dtypes.bfloat16),
     )
@@ -77,14 +77,32 @@
     return mm(table[0], high) + mm(table[0], low) + mm(table[1], high)
 
 
+def apply(d, y):
+    return (
+        d[0] * y[0] + d[1] * y[1] + d[2] * y[2],
+        d[1] * y[0] + d[3] * y[1] + d[4] * y[2],
+        d[2] * y[0] + d[4] * y[1] + d[5] * y[2],
+    )
+
+
+def beside(first_slab, x, prev_row, next_row, column):
+    wide = lax.broadcasted_iota(jnp.int32, (64, AXD), 1)
+    high = lax.broadcasted_iota(jnp.int32, (64, AXD), 0)
+    up = jnp.where(high == 0, prev_row, pltpu.roll(x, 1, 0))
+    down = jnp.where(high == 63, next_row, pltpu.roll(x, 63, 0))
+    left = jnp.where(wide == 0, jnp.where(first_slab, 0.0, column), pltpu.roll(x, 1, 1))
+    right = jnp.where(wide == AXD - 1, jnp.where(first_slab, column, 0.0), pltpu.roll(x, AXD - 1, 1))
+    return up + down + (left + right)
+
+
 def kernel(
     step_hbm, mix_hbm, gain_hbm, traces_hbm, field_hbm, current_hbm, diag_hbm, off_hbm,
     f1_hbm, f2_hbm, g_hbm, h_hbm, tw_hbm, pick_hbm,
-    result,
+    out_a, out_u, out_x, out_d, out_r, out_c,
     step_ref, mix_ref, gain_ref, traces, field, current, diag, off, f1, f2, g, h, tw, pick,
-    dinv, a1, wsend, rrecv, usend, urecv, spec, other, etab,
-    row_s, row_r, col_s, col_r, row2_s, row2_r, col2_s, col2_r, xcol,
-    load, fsend, frecv, usem, ursem, ssend, srecv, hsend, hrecv, h2send, h2recv, xsem,
+    dinv, a1, result, wsend, rrecv, usend, spec, other, etab,
+    row_s, row_r, col_s, col_r, row2_s, row2_r, col2_s, col2_r,
+    load, fsend, frecv, usem, ursem, ssend, srecv, hsend, hrecv, h2send, h2recv, xsem, osem,
 ):
     slab = lax.axis_index("slab")
     me = lax.axis_index("sector")
@@ -113,14 +131,23 @@
 
     barrier = pltpu.get_barrier_semaphore()
 
-    def turn(k):
-        return lax.rem(me + 18 + k, SECTORS)
-
-    def greet(k, carry):
-        pl.semaphore_signal(barrier, inc=1, device_id={"slab": 1 - slab, "sector": turn(k)}, device_id_type=MESH)
-        return carry
-
-    lax.fori_loop(0, SECTORS, greet, 0)
+    mx, mz, my = me >> 5, (me >> 2) & 7, me & 3
+    corners = [x << 5 | (my + d) & 3 for d in (2, 1, 3, 0) for x in (mx, 1 - mx)]
+
+    def each_peer(act):
+        def ring(i, carry):
+            dx = ((i & 1) ^ mx) << 5
+            base = dx | ((my + (i >> 1) + 2) & 3)
+            for dz in (4, 3, 5, 2, 6, 1, 7, 0):
+                act(base | ((mz + dz) & 7) << 2)
+            return carry
+
+        lax.fori_loop(0, 8, ring, 0)
+
+    def greet(j):
+        pl.semaphore_signal(barrier, inc=1, device_id={"slab": 1 - slab, "sector": j}, device_id_type=MESH)
+
+    each_peer(greet)
     pl.semaphore_signal(barrier, inc=1, device_id={"side": 1 - side}, device_id_type=MESH)
     pl.semaphore_signal(barrier, inc=1, device_id={"sector": nxt}, device_id_type=MESH)
     pl.semaphore_signal(barrier, inc=1, device_id={"sector": prv}, device_id_type=MESH)
@@ -137,8 +164,6 @@
         return ref.at[pl.ds(pl.multiple_of(j * 8, 8), 8)]
 
     lane = lax.broadcasted_iota(jnp.int32, (64, 128), 1)
-    wide = lax.broadcasted_iota(jnp.int32, (64, AXD), 1)
-    high = lax.broadcasted_iota(jnp.int32, (64, AXD), 0)
     first_slab = slab == 0
 
     def edge_column(x):
@@ -184,15 +209,13 @@
     for copy in halo1:
         copy.start()
 
-    def scatter(k, carry):
-        j = turn(k)
+    def scatter(j):
         pltpu.make_async_remote_copy(
             src_ref=tile(wsend, j), dst_ref=tile(rrecv, me), send_sem=fsend, recv_sem=frecv,
             device_id={"slab": 1 - slab, "sector": j}, device_id_type=MESH,
         ).start()
-        return carry
-
-    lax.fori_loop(0, SECTORS, scatter, 0)
+
+    each_peer(scatter)
 
     loads[2].wait()
     loads[3].wait()
@@ -216,26 +239,14 @@
     lax.fori_loop(0, LAYERS, invert, 0)
 
     def solve(k, y):
-        d = [dinv[i, k] for i in range(6)]
-        return (
-            d[0] * y[0] + d[1] * y[1] + d[2] * y[2],
-            d[1] * y[0] + d[3] * y[1] + d[4] * y[2],
-            d[2] * y[0] + d[4] * y[1] + d[5] * y[2],
-        )
-
-    def beside(x, prev_row, next_row, column):
-        up = jnp.where(high == 0, prev_row, pltpu.roll(x, 1, 0))
-        down = jnp.where(high == 63, next_row, pltpu.roll(x, 63, 0))
-        left = jnp.where(wide == 0, jnp.where(first_slab, 0.0, column), pltpu.roll(x, 1, 1))
-        right = jnp.where(wide == AXD - 1, jnp.where(first_slab, column, 0.0), pltpu.roll(x, AXD - 1, 1))
-        return up + down + (left + right)
+        return apply([dinv[i, k] for i in range(6)], y)
 
     def relax(k, src, rows_r, cols_r):
         y = []
         for c in range(3):
             x = src[c, k + 1]
             column = pltpu.roll(cols_r[...], 128 - c * 8 - k, 1)[:, 0:1]
-            near = beside(x, rows_r[0, pl.ds(c * 8 + k, 1), :], rows_r[1, pl.ds(c * 8 + k, 1), :], column)
+            near = beside(first_slab, x, rows_r[0, pl.ds(c * 8 + k, 1), :], rows_r[1, pl.ds(c * 8 + k, 1), :], column)
             y.append(current[c, k] + (src[c, k] + src[c, k + 2] + near))
         return solve(k, y)
 
@@ -282,68 +293,87 @@
     sign = (2 * side - 1).astype(F32)
     etab[0] = weight
     etab[1] = scaled * jnp.cos(angle)
-    etab[2] = scaled * jnp.sin(angle) * sign
+    etab[2] = scaled * jnp.sin(angle) * jnp.where(lane % 64 < 32, -sign, sign)
 
     for copy in loads[5:11]:
         copy.wait()
     pltpu.make_async_copy(wsend, rrecv, frecv).wait()
 
     exchange = []
-    for qb in range(2):
-        x = jnp.concatenate([rrecv[pl.ds(2 * r + qb, 64, stride=8), :] for r in range(4)], axis=1)
+    cos_t, sin_t = tw[0], tw[1]
+    left_half = lane < 64
+    real_lane = lane % 64 < 32
+    batch = 2
+    for b in range(2 // batch):
+        order = [(cl, qa, qb) for qb in range(batch * b, batch * b + batch) for cl in range(2) for qa in range(2)]
+        x = jnp.concatenate([rrecv[pl.ds(cl * 4 + qa * 2 + qb, 64, stride=8), :] for cl, qa, qb in order], axis=1)
         y = dot_left(f1, x)
-        cos_t = jnp.concatenate([tw[0]] * 4, axis=1)
-        sin_t = jnp.concatenate([tw[1]] * 4, axis=1)
-        re, im = y[:64], y[64:]
-        t = jnp.concatenate([re * cos_t + im * sin_t, im * cos_t - re * sin_t], axis=1)
-        spec[qb] = dot_right(t, g)
+        rows = []
+        for n in range(4 * batch):
+            re, im = y[:64, n * 128:n * 128 + 128], y[64:, n * 128:n * 128 + 128]
+            rows.append(jnp.concatenate([re * cos_t + im * sin_t, im * cos_t - re * sin_t], axis=1))
+        both = dot_right(jnp.concatenate(rows, axis=0), g)
+        for n in range(2 * batch):
+            spec[2 * batch * b + n] = jnp.where(left_half, both[n * 128:n * 128 + 64], both[n * 128 + 64:n * 128 + 128])
+        part = pl.ds(2 * batch * b, 2 * batch)
         copy = pltpu.make_async_remote_copy(
-            src_ref=spec.at[qb], dst_ref=other.at[qb], send_sem=ssend.at[qb], recv_sem=srecv.at[qb],
+            src_ref=spec.at[part], dst_ref=other.at[part], send_sem=ssend.at[b], recv_sem=srecv.at[b],
             device_id={"side": 1 - side}, device_id_type=MESH,
         )
         copy.start()
         exchange.append(copy)
 
-    left_half = lane < 64
-    for qb in range(2):
-        exchange[qb].wait_recv()
-        sre, sim = spec[qb, :, :128], spec[qb, :, 128:]
-        ore, oim = other[qb, :, :128], other[qb, :, 128:]
-        w, ec, es = etab[0], etab[1], etab[2]
-        c = jnp.concatenate([w * sre + ec * ore - es * oim, w * sim + ec * oim + es * ore], axis=1)
-        z = dot_right(c, h)
-        re, im = z[:, :512], z[:, 512:]
-        cos_t = jnp.concatenate([tw[0]] * 4, axis=1)
-        sin_t = jnp.concatenate([tw[1]] * 4, axis=1)
-        x = dot_left(f2, jnp.concatenate([re * cos_t - im * sin_t, im * cos_t + re * sin_t], axis=0))
-        packed = []
-        for k in range(3):
-            coef = [jnp.where(left_half, mix_ref[k, 0, cl], mix_ref[k, 0, 2 + cl]) for cl in range(2)]
-            mixed = []
-            for qa in range(2):
-                v = coef[0] * x[:, qa * 128:(qa + 1) * 128] + coef[1] * x[:, (2 + qa) * 128:(3 + qa) * 128]
-                mixed.append(v + pltpu.roll(v, 64, 1))
-            packed.append(jnp.where(left_half, mixed[0], mixed[1]))
-            usend[pl.ds(2 * k + qb, 64, stride=8), :] = packed[k]
-        ph, plow = halves(jnp.concatenate(packed, axis=1))
-        ends = mm(ph, pick[...]) + mm(plow, pick[...])
-        usend[pl.ds(6 + qb, 64, stride=8), :] = jnp.where(lane < 8, pltpu.roll(ends, 1, 0), pltpu.roll(ends, 63, 0))
+    for b in range(2 // batch):
+        exchange[b].wait_recv()
+        rows = []
+        for n in range(2 * batch * b, 2 * batch * b + 2 * batch):
+            o = other[n]
+            crossed = jnp.where(real_lane, pltpu.roll(o, 96, 1), pltpu.roll(o, 32, 1))
+            c = etab[0] * spec[n] + etab[1] * o + etab[2] * crossed
+            rows += [c, pltpu.roll(c, 64, 1)]
+        z = dot_right(jnp.concatenate(rows, axis=0), h)
+        parts = []
+        for n in range(4 * batch):
+            re, im = z[n * 64:n * 64 + 64, :128], z[n * 64:n * 64 + 64, 128:]
+            parts.append(jnp.concatenate([re * cos_t - im * sin_t, im * cos_t + re * sin_t], axis=0))
+        wave = dot_left(f2, jnp.concatenate(parts, axis=1))
+        for q in range(batch):
+            qb = b * batch + q
+            packed = []
+            for k in range(3):
+                coef = [jnp.where(left_half, mix_ref[k, 0, cl], mix_ref[k, 0, 2 + cl]) for cl in range(2)]
+                mixed = []
+                for qa in range(2):
+                    at = [(q * 4 + cl * 2 + qa) * 128 for cl in range(2)]
+                    v = coef[0] * wave[:, at[0]:at[0] + 128] + coef[1] * wave[:, at[1]:at[1] + 128]
+                    mixed.append(v + pltpu.roll(v, 64, 1))
+                packed.append(jnp.where(left_half, mixed[0], mixed[1]))
+                usend[pl.ds(2 * k + qb, 64, stride=8), :] = packed[k]
+            ph, plow = halves(jnp.concatenate(packed, axis=1))
+            ends = mm(ph, pick[...]) + mm(plow, pick[...])
+            usend[pl.ds(6 + qb, 64, stride=8), :] = jnp.where(lane < 8, pltpu.roll(ends, 1, 0), pltpu.roll(ends, 63, 0))
 
     special = jnp.where(first_slab, SECTORS - 1, 0)
     mine = jnp.where(me == SECTORS - 1 - special, 1, 0)
 
-    def gather(k, carry):
-        j = turn(k)
+    def gather(j):
         pltpu.make_async_remote_copy(
-            src_ref=tile(usend, j), dst_ref=tile(urecv, me), send_sem=usem, recv_sem=ursem.at[mine],
+            src_ref=tile(usend, j), dst_ref=tile(out_u, me), send_sem=usem, recv_sem=ursem.at[mine],
             device_id={"slab": 1 - slab, "sector": j}, device_id_type=MESH,
         ).start()
-        return carry
-
-    lax.fori_loop(0, SECTORS, gather, 0)
+
+    each_peer(gather)
 
     for copy in halo2:
         copy.wait_recv()
+    outs = [
+        pltpu.make_async_copy(dinv.at[:, pl.ds(0, 2)], out_d, osem.at[0]),
+        pltpu.make_async_copy(row2_r, out_r, osem.at[1]),
+        pltpu.make_async_copy(col2_r, out_c, osem.at[2]),
+        pltpu.make_async_copy(result, out_a, osem.at[3]),
+    ]
+    for copy in outs[:3]:
+        copy.start()
 
     def sweep2(k, carry):
         new = relax(k, a1, row2_r, col2_r)
@@ -352,14 +382,44 @@
         return carry
 
     lax.fori_loop(0, LAYERS, sweep2, 0)
-
-    pltpu.make_async_copy(tile(usend, 0), tile(urecv, 0), ursem.at[1]).wait()
+    outs[3].start()
+
+    pltpu.make_async_copy(tile(usend, 0), tile(out_u, 0), ursem.at[1]).wait()
     forward = pltpu.make_async_remote_copy(
-        src_ref=tile(urecv, special), dst_ref=xcol, send_sem=xsem.at[0], recv_sem=xsem.at[1],
+        src_ref=tile(out_u, special), dst_ref=out_x, send_sem=xsem.at[0], recv_sem=xsem.at[1],
         device_id={"slab": 1 - slab}, device_id_type=MESH,
     )
     forward.start()
-    pltpu.make_async_copy(usend.at[pl.ds(0, 504)], urecv.at[pl.ds(0, 504)], ursem.at[0]).wait()
+    pltpu.make_async_copy(usend.at[pl.ds(0, 504)], out_u.at[pl.ds(0, 504)], ursem.at[0]).wait()
+
+    forward.wait_recv()
+    pltpu.make_async_copy(wsend, rrecv, fsend).wait()
+    pltpu.make_async_copy(usend, out_u, usem).wait()
+    for copy in outs:
+        copy.wait()
+    for copy in halo1 + halo2 + exchange + [forward]:
+        copy.wait_send()
+
+
+def finish(a_hbm, u_hbm, x_hbm, d_hbm, r_hbm, c_hbm, out, result, urecv, xcol, dinv, rows, cols_r, isem, osem):
+    first_slab = lax.axis_index("slab") == 0
+    loads = [
+        pltpu.make_async_copy(src, dst, isem.at[i])
+        for i, (src, dst) in enumerate(((u_hbm, urecv), (d_hbm, dinv), (x_hbm, xcol), (r_hbm, rows), (c_hbm, cols_r)))
+    ]
+    layers = [pl.ds(k, 2) for k in range(0, LAYERS, 2)]
+    loads += [pltpu.make_async_copy(a_hbm.at[:, k], result.at[:, k], isem.at[5 + i]) for i, k in enumerate(layers)]
+    stores = [pltpu.make_async_copy(result.at[:, k], out.at[:, k], osem.at[i]) for i, k in enumerate(layers)]
+    for copy in loads:
+        copy.start()
+    for i in range(1, 4):
+        loads[5 + i].wait()
+        stores[i].start()
+    for copy in loads[:6]:
+        copy.wait()
+
+    def solve(k, y):
+        return apply([dinv[i, k] for i in range(6)], y)
 
     turned = []
     for k in range(4):
@@ -370,58 +430,47 @@
     src_next = [jnp.concatenate([turned[3][8 + c:9 + c], turned[3][12 + c:13 + c]], axis=1) for c in range(3)]
     delta = solve(0, source)
 
-    def apply(d, y):
-        return (
-            d[0] * y[0] + d[1] * y[1] + d[2] * y[2],
-            d[1] * y[0] + d[3] * y[1] + d[4] * y[2],
-            d[2] * y[0] + d[4] * y[1] + d[5] * y[2],
-        )
-
-    delta_prev = apply([row2_r[0, 24 + i:25 + i, :] for i in range(6)], src_prev)
-    delta_next = apply([row2_r[1, 24 + i:25 + i, :] for i in range(6)], src_next)
-    forward.wait_recv()
+    delta_prev = apply([rows[0, 24 + i:25 + i, :] for i in range(6)], src_prev)
+    delta_next = apply([rows[1, 24 + i:25 + i, :] for i in range(6)], src_next)
     cols = xcol[...].T
     cols = [jnp.where(first_slab, cols[:64, 2 * c:2 * c + 1], cols[64:, 2 * c + 1:2 * c + 2]) for c in range(3)]
-    dcol = col2_r[...]
+    dcol = cols_r[...]
     delta_col = apply([dcol[:, 24 + i:25 + i] for i in range(6)], cols)
-    y = [source[c] + beside(delta[c], delta_prev[c], delta_next[c], delta_col[c]) for c in range(3)]
+    y = [source[c] + beside(first_slab, delta[c], delta_prev[c], delta_next[c], delta_col[c]) for c in range(3)]
     low = solve(0, y)
     up = solve(1, delta)
     for c in range(3):
         result[c, 0] = result[c, 0] + low[c]
         result[c, 1] = result[c, 1] + up[c]
-
-    pltpu.make_async_copy(wsend, rrecv, fsend).wait()
-    pltpu.make_async_copy(usend, urecv, usem).wait()
-    for copy in halo1 + halo2 + exchange + [forward]:
-        copy.wait_send()
+    stores[0].start()
+    for copy in stores:
+        copy.wait()
 
 
 def shards(traces, gap_gain, rotor_step, mixing, field, current, cond_diag, cond_off):
     consts = [jnp.asarray(t) for t in tables()]
     hbm = pl.BlockSpec(memory_space=pltpu.HBM)
-    vmem = pl.BlockSpec(memory_space=pltpu.VMEM)
     block = (3, LAYERS, PHD, AXD)
     dma = pltpu.SemaphoreType.DMA
     v = pltpu.VMEM
-    out = pl.pallas_call(
+    shapes = (block, (512, 128), (8, 128), (6, 2, 64, AXD), (2, 32, AXD), (64, 128))
+    parts = pl.pallas_call(
         kernel,
-        out_shape=jax.ShapeDtypeStruct(block, F32),
+        out_shape=[jax.ShapeDtypeStruct(shape, F32) for shape in shapes],
         in_specs=[hbm] * 14,
-        out_specs=vmem,
+        out_specs=[hbm] * 6,
         scratch_shapes=[
             pltpu.SMEM((1,), jnp.int32), pltpu.SMEM((3, 1, 4), F32), v((8, 128), F32),
             v((64, 4, AXD), F32), v((3, LAYERS + 2, 64, AXD), F32), v(block, F32), v(block, F32), v(block, F32),
-            v((2, 128, 64), BF16), v((2, 64, 128), BF16), v((2, 1024, 256), BF16), v((2, 256, 1024), BF16),
+            v((2, 128, 64), BF16), v((2, 64, 128), BF16), v((2, 256, 128), BF16), v((2, 128, 256), BF16),
             v((2, 64, 128), F32), v((384, 128), BF16),
-            v((6, LAYERS, 64, AXD), F32), v((3, LAYERS + 2, 64, AXD), F32),
-            v((512, 128), F32), v((512, 128), F32), v((512, 128), F32), v((512, 128), F32),
-            v((2, 64, 256), F32), v((2, 64, 256), F32), v((3, 64, 128), F32),
+            v((6, LAYERS, 64, AXD), F32), v((3, LAYERS + 2, 64, AXD), F32), v(block, F32),
+            v((512, 128), F32), v((512, 128), F32), v((512, 128), F32),
+            v((4, 64, 128), F32), v((4, 64, 128), F32), v((3, 64, 128), F32),
             v((2, 24, AXD), F32), v((2, 24, AXD), F32), v((64, 128), F32), v((64, 128), F32),
             v((2, 32, AXD), F32), v((2, 32, AXD), F32), v((64, 128), F32), v((64, 128), F32),
-            v((8, 128), F32),
-            dma((14,)), dma, dma, dma, dma((2,)), dma((2,)), dma((2,)),
-            dma((3,)), dma((3,)), dma((3,)), dma((3,)), dma((2,)),
+            dma((14,)), dma, dma, dma, dma((2,)), dma((4,)), dma((4,)),
+            dma((3,)), dma((3,)), dma((3,)), dma((3,)), dma((2,)), dma((4,)),
         ],
         compiler_params=pltpu.CompilerParams(collective_id=0, has_side_effects=True, vmem_limit_bytes=62 * 1024 * 1024),
         cost_estimate=pl.CostEstimate(flops=400_000_000, bytes_accessed=10_000_000, transcendentals=0),
@@ -429,6 +478,15 @@
         rotor_step, jnp.transpose(mixing, (1, 0, 2)), gap_gain.reshape(8, 128), traces[0], field[0], current[0], cond_diag[0], cond_off[0],
         *consts,
     )
+    out = pl.pallas_call(
+        finish,
+        out_shape=jax.ShapeDtypeStruct(block, F32),
+        in_specs=[hbm] * 6,
+        out_specs=hbm,
+        scratch_shapes=[v(shape, F32) for shape in shapes] + [dma((9,)), dma((4,))],
+        compiler_params=pltpu.CompilerParams(vmem_limit_bytes=62 * 1024 * 1024),
+        cost_estimate=pl.CostEstimate(flops=10_000_000, bytes_accessed=4_200_000, transcendentals=0),
+    )(*parts)
     return out[None]
 
 

time: 44.4 us -> 42.3 us (0.953)
  local copies, waits for them, and re-layouts: 2.7 us -> 0 us
    unnamed x1 -> x0, local copies, waits for them, and re-layouts: 2.7 us -> none
    pallas_call x1 -> x2, Pallas kernels: 40.9 us -> 41.2 us  [the longest x1 37.9 us: shards(): pl.pallas_call(kernel, out_shape=[jax.ShapeDtypeStruct(shape, F32) for sh...]
where the time goes in v3:
time: 42.3 us; the launch traced here: 41.8 us
  Pallas kernels  41.2 us (97%)
  between operations  0.66 us (2%)
    pallas_call x1, Pallas kernels, shards(): pl.pallas_call(kernel, out_shape=[jax.ShapeDtypeStruct(shape, F32) for sh...  37.9 us
    pallas_call x1, Pallas kernels, shards(): pl.pallas_call(finish, out_shape=jax.ShapeDtypeStruct(block, F32), in_spe...  3.21 us

profile of v3, /device:TPU:1, one launch (start us, length us, event | category | flops | bytes accessed | tf_op | source)
XLA Modules:
  0.0 41.8 jit_solution(14778123616196943178)
XLA Ops:
  0.7 37.9 %shard_map.136 = (f32[3,8,64,256]{3,2,1,0:T(8,128)}, f32[512,128]{1,0:T(8,128)}, f32[8,128]{1,0:T(8,128)}, f32[6,2,64,256]{3,2,1,0:T(8,128)}, f32[2,32,256]{2,1,0:T(8,128)}, /*index=5*/f32[64,128]{1,0:T(8,128)}) custom-call(s32[1]{0:T(128)S(6)} %copy.15.step_hbm, f32[3,1,4]{2,1,0:T(1,128)} %bitcast.14, f32[8,128]{1,0:T(8,128)} %bitcast.13, ...), custom_call_target="tpu_custom_call" | custom-call | flops 400000000 | bytes 10000000 | tf_op jit(solution)/shard_map/pallas_call | solution.py:457
  38.6 3.2 %shard_map.137 = f32[3,8,64,256]{3,2,1,0:T(8,128)} custom-call(f32[3,8,64,256]{3,2,1,0:T(8,128)} %get-tuple-element.11.a_hbm, f32[512,128]{1,0:T(8,128)} %get-tuple-element.12.u_hbm, f32[8,128]{1,0:T(8,128)} %get-tuple-element.13.x_hbm, f32[6,2,64,256]{3,2,1,0:T(8,128)} %get-tuple-element.14.d_hbm, f32[2,32,256]{2,1,0:T(8,128)} %get-tuple-element.15.r_hbm, ...), custom_call_target="tpu_custom_call" | custom-call | flops 10000000 | bytes 4200000 | tf_op jit(solution)/shard_map/pallas_call | solution.py:481

commit v4 on v3

--- a/solution.py
+++ b/solution.py
@@ -160,8 +160,8 @@
             for qb in range(2):
                 wsend[pl.ds(cl * 4 + qa * 2 + qb, 64, stride=8), :] = turned[qb * 64:(qb + 1) * 64]
 
-    def tile(ref, j):
-        return ref.at[pl.ds(pl.multiple_of(j * 8, 8), 8)]
+    def tile(ref, j, rows=8):
+        return ref.at[pl.ds(pl.multiple_of(j * 8, 8), rows)]
 
     lane = lax.broadcasted_iota(jnp.int32, (64, 128), 1)
     first_slab = slab == 0
@@ -274,15 +274,13 @@
         columns = jnp.where(lane == 24 + i, edge_column(x), columns)
     col2_s[...] = columns
     halo2 = halo(row2_s, row2_r, col2_s, col2_r, h2send, h2recv)
-    for copy in halo2:
-        copy.start()
 
     for copy in loads[11:]:
         copy.wait()
 
     m1 = lane % M1
     harm = lax.broadcasted_iota(jnp.int32, (64, 128), 0) + 64 * m1
-    angle = (harm * step_ref[0] % NPHI).astype(F32) * (2.0 * math.pi / NPHI)
+    angle = (harm * step_ref[0, 0] % NPHI).astype(F32) * (2.0 * math.pi / NPHI)
     weight = jnp.where(harm == 0, 1.0 / NPHI, 2.0 / NPHI)
     turned = gain_ref[...].T
     gain = jnp.zeros((64, 128), F32)
@@ -298,8 +296,11 @@
     for copy in loads[5:11]:
         copy.wait()
     pltpu.make_async_copy(wsend, rrecv, frecv).wait()
+    for copy in halo2:
+        copy.start()
 
     exchange = []
+    edge = []
     cos_t, sin_t = tw[0], tw[1]
     left_half = lane < 64
     real_lane = lane % 64 < 32
@@ -351,14 +352,16 @@
                 usend[pl.ds(2 * k + qb, 64, stride=8), :] = packed[k]
             ph, plow = halves(jnp.concatenate(packed, axis=1))
             ends = mm(ph, pick[...]) + mm(plow, pick[...])
-            usend[pl.ds(6 + qb, 64, stride=8), :] = jnp.where(lane < 8, pltpu.roll(ends, 1, 0), pltpu.roll(ends, 63, 0))
+            edge.append(jnp.where(lane & 8 == 0, pltpu.roll(ends, 1, 0), pltpu.roll(ends, 63, 0)))
+
+    usend[pl.ds(6, 64, stride=8), :] = jnp.where(lane < 16, edge[0], pltpu.roll(edge[1], 16, 1))
 
     special = jnp.where(first_slab, SECTORS - 1, 0)
     mine = jnp.where(me == SECTORS - 1 - special, 1, 0)
 
     def gather(j):
         pltpu.make_async_remote_copy(
-            src_ref=tile(usend, j), dst_ref=tile(out_u, me), send_sem=usem, recv_sem=ursem.at[mine],
+            src_ref=tile(usend, j, 7), dst_ref=tile(out_u, me, 7), send_sem=usem, recv_sem=ursem.at[mine],
             device_id={"slab": 1 - slab, "sector": j}, device_id_type=MESH,
         ).start()
 
@@ -384,17 +387,17 @@
     lax.fori_loop(0, LAYERS, sweep2, 0)
     outs[3].start()
 
-    pltpu.make_async_copy(tile(usend, 0), tile(out_u, 0), ursem.at[1]).wait()
+    pltpu.make_async_copy(tile(usend, 0, 7), tile(out_u, 0, 7), ursem.at[1]).wait()
     forward = pltpu.make_async_remote_copy(
-        src_ref=tile(out_u, special), dst_ref=out_x, send_sem=xsem.at[0], recv_sem=xsem.at[1],
+        src_ref=tile(out_u, special, 7), dst_ref=out_x.at[pl.ds(0, 7)], send_sem=xsem.at[0], recv_sem=xsem.at[1],
         device_id={"slab": 1 - slab}, device_id_type=MESH,
     )
     forward.start()
-    pltpu.make_async_copy(usend.at[pl.ds(0, 504)], out_u.at[pl.ds(0, 504)], ursem.at[0]).wait()
+    pltpu.make_async_copy(usend.at[pl.ds(0, 441)], out_u.at[pl.ds(0, 441)], ursem.at[0]).wait()
 
     forward.wait_recv()
     pltpu.make_async_copy(wsend, rrecv, fsend).wait()
-    pltpu.make_async_copy(usend, out_u, usem).wait()
+    pltpu.make_async_copy(usend.at[pl.ds(0, 448)], out_u.at[pl.ds(0, 448)], usem).wait()
     for copy in outs:
         copy.wait()
     for copy in halo1 + halo2 + exchange + [forward]:
@@ -422,9 +425,11 @@
         return apply([dinv[i, k] for i in range(6)], y)
 
     turned = []
-    for k in range(4):
+    for k in range(3):
         both = jnp.concatenate([urecv[pl.ds(2 * k + qb, 64, stride=8), :] for qb in range(2)], axis=0)
         turned.append(both.T)
+    edge = urecv[pl.ds(6, 64, stride=8), :]
+    turned.append(jnp.concatenate([edge, pltpu.roll(edge, 112, 1)], axis=0).T)
     source = [jnp.concatenate([turned[c][:64], turned[c][64:]], axis=1) for c in range(3)]
     src_prev = [jnp.concatenate([turned[3][c:c + 1], turned[3][4 + c:5 + c]], axis=1) for c in range(3)]
     src_next = [jnp.concatenate([turned[3][8 + c:9 + c], turned[3][12 + c:13 + c]], axis=1) for c in range(3)]
@@ -460,7 +465,7 @@
         in_specs=[hbm] * 14,
         out_specs=[hbm] * 6,
         scratch_shapes=[
-            pltpu.SMEM((1,), jnp.int32), pltpu.SMEM((3, 1, 4), F32), v((8, 128), F32),
+            pltpu.SMEM((1, 1), jnp.int32), pltpu.SMEM((3, 1, 4), F32), v((8, 128), F32),
             v((64, 4, AXD), F32), v((3, LAYERS + 2, 64, AXD), F32), v(block, F32), v(block, F32), v(block, F32),
             v((2, 128, 64), BF16), v((2, 64, 128), BF16), v((2, 256, 128), BF16), v((2, 128, 256), BF16),
             v((2, 64, 128), F32), v((384, 128), BF16),
@@ -475,7 +480,7 @@
         compiler_params=pltpu.CompilerParams(collective_id=0, has_side_effects=True, vmem_limit_bytes=62 * 1024 * 1024),
         cost_estimate=pl.CostEstimate(flops=400_000_000, bytes_accessed=10_000_000, transcendentals=0),
     )(
-        rotor_step, jnp.transpose(mixing, (1, 0, 2)), gap_gain.reshape(8, 128), traces[0], field[0], current[0], cond_diag[0], cond_off[0],
+        rotor_step.reshape(1, 1), jnp.transpose(mixing, (1, 0, 2)), gap_gain.reshape(8, 128), traces[0], field[0], current[0], cond_diag[0], cond_off[0],
         *consts,
     )
     out = pl.pallas_call(

time: 42.3 us -> 41.7 us (0.986)
  Pallas kernels: 41.2 us -> 40.6 us
    pallas_call x1, Pallas kernels: 37.9 us -> 37.3 us  [shards(): pl.pallas_call(kernel, out_shape=[jax.ShapeDtypeStruct(shape, F32) for sh...]
where the time goes in v4:
time: 41.7 us; the launch traced here: 41.2 us
  Pallas kernels  40.6 us (97%)
  between operations  0.66 us (2%)
    pallas_call x1, Pallas kernels, shards(): pl.pallas_call(kernel, out_shape=[jax.ShapeDtypeStruct(shape, F32) for sh...  37.3 us
    pallas_call x1, Pallas kernels, shards(): pl.pallas_call(finish, out_shape=jax.ShapeDtypeStruct(block, F32), in_spe...  3.27 us

profile of v4, /device:TPU:1, one launch (start us, length us, event | category | flops | bytes accessed | tf_op | source)
XLA Modules:
  0.0 41.2 jit_solution(14813988108324814595)
XLA Ops:
  0.7 37.3 %shard_map.136 = (f32[3,8,64,256]{3,2,1,0:T(8,128)}, f32[512,128]{1,0:T(8,128)}, f32[8,128]{1,0:T(8,128)}, f32[6,2,64,256]{3,2,1,0:T(8,128)}, f32[2,32,256]{2,1,0:T(8,128)}, /*index=5*/f32[64,128]{1,0:T(8,128)}) custom-call(s32[1,1]{1,0:T(1,128)} %bitcast.9.step_hbm, f32[3,1,4]{2,1,0:T(1,128)} %bitcast.16, f32[8,128]{1,0:T(8,128)} %bitcast.15, ...), custom_call_target="tpu_custom_call" | custom-call | flops 400000000 | bytes 10000000 | tf_op jit(solution)/shard_map/pallas_call | solution.py:462
  37.9 3.3 %shard_map.137 = f32[3,8,64,256]{3,2,1,0:T(8,128)} custom-call(f32[3,8,64,256]{3,2,1,0:T(8,128)} %get-tuple-element.11.a_hbm, f32[512,128]{1,0:T(8,128)} %get-tuple-element.12.u_hbm, f32[8,128]{1,0:T(8,128)} %get-tuple-element.13.x_hbm, f32[6,2,64,256]{3,2,1,0:T(8,128)} %get-tuple-element.14.d_hbm, f32[2,32,256]{2,1,0:T(8,128)} %get-tuple-element.15.r_hbm, ...), custom_call_target="tpu_custom_call" | custom-call | flops 10000000 | bytes 4200000 | tf_op jit(solution)/shard_map/pallas_call | solution.py:486

commit v5 on v4

--- a/solution.py
+++ b/solution.py
@@ -136,10 +136,8 @@
 
     def each_peer(act):
         def ring(i, carry):
-            dx = ((i & 1) ^ mx) << 5
-            base = dx | ((my + (i >> 1) + 2) & 3)
-            for dz in (4, 3, 5, 2, 6, 1, 7, 0):
-                act(base | ((mz + dz) & 7) << 2)
+            for k in range(8):
+                act((me + 18 + 8 * i + k) & 63)
             return carry
 
         lax.fori_loop(0, 8, ring, 0)
@@ -410,20 +408,16 @@
         pltpu.make_async_copy(src, dst, isem.at[i])
         for i, (src, dst) in enumerate(((u_hbm, urecv), (d_hbm, dinv), (x_hbm, xcol), (r_hbm, rows), (c_hbm, cols_r)))
     ]
-    layers = [pl.ds(k, 2) for k in range(0, LAYERS, 2)]
+    layers = [pl.ds(0, 1), pl.ds(1, 1), pl.ds(2, 2), pl.ds(4, 2), pl.ds(6, 2)]
     loads += [pltpu.make_async_copy(a_hbm.at[:, k], result.at[:, k], isem.at[5 + i]) for i, k in enumerate(layers)]
     stores = [pltpu.make_async_copy(result.at[:, k], out.at[:, k], osem.at[i]) for i, k in enumerate(layers)]
     for copy in loads:
         copy.start()
-    for i in range(1, 4):
-        loads[5 + i].wait()
-        stores[i].start()
-    for copy in loads[:6]:
-        copy.wait()
 
     def solve(k, y):
         return apply([dinv[i, k] for i in range(6)], y)
 
+    loads[0].wait()
     turned = []
     for k in range(3):
         both = jnp.concatenate([urecv[pl.ds(2 * k + qb, 64, stride=8), :] for qb in range(2)], axis=0)
@@ -433,7 +427,18 @@
     source = [jnp.concatenate([turned[c][:64], turned[c][64:]], axis=1) for c in range(3)]
     src_prev = [jnp.concatenate([turned[3][c:c + 1], turned[3][4 + c:5 + c]], axis=1) for c in range(3)]
     src_next = [jnp.concatenate([turned[3][8 + c:9 + c], turned[3][12 + c:13 + c]], axis=1) for c in range(3)]
+    loads[1].wait()
     delta = solve(0, source)
+    up = solve(1, delta)
+    loads[6].wait()
+    for c in range(3):
+        result[c, 1] = result[c, 1] + up[c]
+    stores[1].start()
+    for i in range(2, 5):
+        loads[5 + i].wait()
+        stores[i].start()
+    for copy in loads[2:6]:
+        copy.wait()
 
     delta_prev = apply([rows[0, 24 + i:25 + i, :] for i in range(6)], src_prev)
     delta_next = apply([rows[1, 24 + i:25 + i, :] for i in range(6)], src_next)
@@ -443,10 +448,8 @@
     delta_col = apply([dcol[:, 24 + i:25 + i] for i in range(6)], cols)
     y = [source[c] + beside(first_slab, delta[c], delta_prev[c], delta_next[c], delta_col[c]) for c in range(3)]
     low = solve(0, y)
-    up = solve(1, delta)
     for c in range(3):
         result[c, 0] = result[c, 0] + low[c]
-        result[c, 1] = result[c, 1] + up[c]
     stores[0].start()
     for copy in stores:
         copy.wait()
@@ -488,7 +491,7 @@
         out_shape=jax.ShapeDtypeStruct(block, F32),
         in_specs=[hbm] * 6,
         out_specs=hbm,
-        scratch_shapes=[v(shape, F32) for shape in shapes] + [dma((9,)), dma((4,))],
+        scratch_shapes=[v(shape, F32) for shape in shapes] + [dma((10,)), dma((5,))],
         compiler_params=pltpu.CompilerParams(vmem_limit_bytes=62 * 1024 * 1024),
         cost_estimate=pl.CostEstimate(flops=10_000_000, bytes_accessed=4_200_000, transcendentals=0),
     )(*parts)

time: 41.7 us -> 40.9 us (0.981)
  Pallas kernels: 40.6 us -> 40 us
where the time goes in v5:
time: 40.9 us; the launch traced here: 40.7 us
  Pallas kernels  40 us (98%)
  between operations  0.66 us (2%)
    pallas_call x1, Pallas kernels, shards(): pl.pallas_call(kernel, out_shape=[jax.ShapeDtypeStruct(shape, F32) for sh...  37 us
    pallas_call x1, Pallas kernels, shards(): pl.pallas_call(finish, out_shape=jax.ShapeDtypeStruct(block, F32), in_spe...  3.02 us

profile of v5, /device:TPU:1, one launch (start us, length us, event | category | flops | bytes accessed | tf_op | source)
XLA Modules:
  0.0 40.7 jit_solution(4443567274612059209)
XLA Ops:
  0.7 37.0 %shard_map.136 = (f32[3,8,64,256]{3,2,1,0:T(8,128)}, f32[512,128]{1,0:T(8,128)}, f32[8,128]{1,0:T(8,128)}, f32[6,2,64,256]{3,2,1,0:T(8,128)}, f32[2,32,256]{2,1,0:T(8,128)}, /*index=5*/f32[64,128]{1,0:T(8,128)}) custom-call(s32[1,1]{1,0:T(1,128)} %bitcast.9.step_hbm, f32[3,1,4]{2,1,0:T(1,128)} %bitcast.16, f32[8,128]{1,0:T(8,128)} %bitcast.15, ...), custom_call_target="tpu_custom_call" | custom-call | flops 400000000 | bytes 10000000 | tf_op jit(solution)/shard_map/pallas_call | solution.py:465
  37.7 3.0 %shard_map.137 = f32[3,8,64,256]{3,2,1,0:T(8,128)} custom-call(f32[3,8,64,256]{3,2,1,0:T(8,128)} %get-tuple-element.11.a_hbm, f32[512,128]{1,0:T(8,128)} %get-tuple-element.12.u_hbm, f32[8,128]{1,0:T(8,128)} %get-tuple-element.13.x_hbm, f32[6,2,64,256]{3,2,1,0:T(8,128)} %get-tuple-element.14.d_hbm, f32[2,32,256]{2,1,0:T(8,128)} %get-tuple-element.15.r_hbm, ...), custom_call_target="tpu_custom_call" | custom-call | flops 10000000 | bytes 4200000 | tf_op jit(solution)/shard_map/pallas_call | solution.py:489

commit v6 on v5

--- a/solution.py
+++ b/solution.py
@@ -137,7 +137,7 @@
     def each_peer(act):
         def ring(i, carry):
             for k in range(8):
-                act((me + 18 + 8 * i + k) & 63)
+                act((me + 8 * i + k) & 63)
             return carry
 
         lax.fori_loop(0, 8, ring, 0)

time: 40.9 us -> 39.9 us (0.976)
  Pallas kernels: 40 us -> 39.1 us
    pallas_call x1, Pallas kernels: 37 us -> 36.1 us  [shards(): pl.pallas_call(kernel, out_shape=[jax.ShapeDtypeStruct(shape, F32) for sh...]
where the time goes in v6:
time: 39.9 us; the launch traced here: 39.8 us
  Pallas kernels  39.1 us (98%)
  between operations  0.66 us (2%)
    pallas_call x1, Pallas kernels, shards(): pl.pallas_call(kernel, out_shape=[jax.ShapeDtypeStruct(shape, F32) for sh...  36.1 us
    pallas_call x1, Pallas kernels, shards(): pl.pallas_call(finish, out_shape=jax.ShapeDtypeStruct(block, F32), in_spe...  3.02 us

profile of v6, /device:TPU:1, one launch (start us, length us, event | category | flops | bytes accessed | tf_op | source)
XLA Modules:
  0.0 39.8 jit_solution(14853088846477822561)
XLA Ops:
  0.7 36.1 %shard_map.136 = (f32[3,8,64,256]{3,2,1,0:T(8,128)}, f32[512,128]{1,0:T(8,128)}, f32[8,128]{1,0:T(8,128)}, f32[6,2,64,256]{3,2,1,0:T(8,128)}, f32[2,32,256]{2,1,0:T(8,128)}, /*index=5*/f32[64,128]{1,0:T(8,128)}) custom-call(s32[1,1]{1,0:T(1,128)} %bitcast.9.step_hbm, f32[3,1,4]{2,1,0:T(1,128)} %bitcast.16, f32[8,128]{1,0:T(8,128)} %bitcast.15, ...), custom_call_target="tpu_custom_call" | custom-call | flops 400000000 | bytes 10000000 | tf_op jit(solution)/shard_map/pallas_call | solution.py:465
  36.8 3.0 %shard_map.137 = f32[3,8,64,256]{3,2,1,0:T(8,128)} custom-call(f32[3,8,64,256]{3,2,1,0:T(8,128)} %get-tuple-element.11.a_hbm, f32[512,128]{1,0:T(8,128)} %get-tuple-element.12.u_hbm, f32[8,128]{1,0:T(8,128)} %get-tuple-element.13.x_hbm, f32[6,2,64,256]{3,2,1,0:T(8,128)} %get-tuple-element.14.d_hbm, f32[2,32,256]{2,1,0:T(8,128)} %get-tuple-element.15.r_hbm, ...), custom_call_target="tpu_custom_call" | custom-call | flops 10000000 | bytes 4200000 | tf_op jit(solution)/shard_map/pallas_call | solution.py:489
